TPU v7x, 512 devices: a whole 4x4x16 slice. The times are simulated.
512 devices in a mesh: batch: 128 (over z, y, core), grp: 4 (over x).
Axes of the slice: x: 4, y: 4, z: 16, core: 2. Of those that a mesh axis runs over, the one named last changes fastest.
Arguments:
- queries: bfloat16 [65536, 4096], P(('batch', 'grp')), may hold values from -16 to 16
- passages: bfloat16 [65536, 4096], P(('batch', 'grp')), may hold values from -16 to 16
- hard_ids: int32 [65536], P(('batch', 'grp')), may hold values from 0 to 16383, as said below
Outputs:
- query_grad: bfloat16 [65536, 4096], P(('batch', 'grp'))
- passage_grad: bfloat16 [65536, 4096], P(('batch', 'grp'))
Inputs may be any that keep to these rules, and one draw needn't show every extreme that they name: `hard_ids`: an entry v names the passage at offset v % 128 of the device with batch index v // 128 and the query's grp index; the queries of one device name at most 2 rows held by any one device, exactly 2 on some device, and in every grp index some device is named 2 times by every device of that grp index.
All inputs are finite; a program needn't handle non-finite values.
Results may differ from a plain program's by a relative error of at most 0.0095.
Values may be sent and summed in bfloat16 or wider, within the bound.
A program may use at most 64 MiB of HBM per device.

v0:
```python
import jax
import jax.numpy as jnp
from jax import lax
from jax.sharding import PartitionSpec as P

SOFTMAX_TEMPER = 0.02
LOSS_SCALE = 64.0
EPSILON = 1e-06


def row_scales(values):
    floats = values.astype(jnp.float32)
    return lax.rsqrt(jnp.mean(floats * floats, -1, keepdims=True) + EPSILON)


def norm_back(values, scales, upstream):
    floats = values.astype(jnp.float32)
    return scales * upstream - scales * scales * scales * floats * jnp.mean(
        floats * upstream, -1, keepdims=True
    )


def local(queries, passages, hard_ids):
    pair_rows, embedding_dimension = queries.shape
    batch_count = lax.axis_size("batch")
    group_number_total = lax.axis_size("grp")
    group_pos = lax.axis_index("grp")
    capacity = 2 * ((pair_rows + batch_count - 1) // batch_count)
    slot_total = batch_count * capacity
    group_rows = group_number_total * pair_rows
    inverse_permutation = 1.0 / (embedding_dimension * SOFTMAX_TEMPER)
    factor = LOSS_SCALE * inverse_permutation
    qscale = row_scales(queries)
    pscale = row_scales(passages)
    qshort = (queries.astype(jnp.float32) * qscale).astype(jnp.bfloat16)
    pshort = (passages.astype(jnp.float32) * pscale).astype(jnp.bfloat16)
    owners = hard_ids // pair_rows
    offsets = hard_ids % pair_rows
    local_rows = jnp.arange(pair_rows)
    same_owner = owners[:, None] == owners[None, :]
    earlier = local_rows[:, None] > local_rows[None, :]
    rank_in = jnp.sum((same_owner & earlier).astype(jnp.int32), 1)
    slot_index = owners * capacity + rank_in
    slot_table = jnp.arange(slot_total)[:, None] == slot_index[None, :]
    requests = jnp.sum(jnp.where(slot_table, offsets[None, :], 0), 1)
    requests = requests.reshape(batch_count, capacity)
    served_req = lax.all_to_all(requests, "batch", split_axis=0, concat_axis=0, tiled=True)
    served_flat = served_req.reshape(-1)
    served = jnp.take(pshort, served_flat, axis=0).reshape(
        batch_count, capacity, embedding_dimension
    )
    arrived = lax.all_to_all(served, "batch", split_axis=0, concat_axis=0, tiled=True)
    hard_p = jnp.take(arrived.reshape(slot_total, embedding_dimension), slot_index, axis=0)
    group_p, group_q = (
        lax.all_gather(pshort, "grp", axis=0, tiled=True),
        lax.all_gather(qshort, "grp", axis=0, tiled=True),
    )
    own_cols = group_pos * pair_rows + local_rows
    positive = (jnp.arange(group_rows)[None, :] == own_cols[:, None]).astype(jnp.float32)
    inner_scores = (
        jnp.dot(qshort, group_p.T, preferred_element_type=jnp.float32) * inverse_permutation
    )
    hard_score = (
        jnp.einsum("rd,rd->r", qshort, hard_p, preferred_element_type=jnp.float32)
        * inverse_permutation
    )
    totals = jnp.log(jnp.sum(jnp.exp(inner_scores), 1) + jnp.exp(hard_score))
    inner_w = (jnp.exp(inner_scores - totals[:, None]) - positive).astype(jnp.bfloat16)
    hard_w = jnp.exp(hard_score - totals).astype(jnp.bfloat16)
    unit_q = (
        jnp.dot(inner_w, group_p, preferred_element_type=jnp.float32)
        + hard_w.astype(jnp.float32)[:, None] * hard_p
    ) * factor
    query_grad = norm_back(queries, qscale, unit_q).astype(jnp.bfloat16)
    group_totals = lax.all_gather(totals, "grp", axis=0, tiled=True)
    scores = jnp.dot(group_q, pshort.T, preferred_element_type=jnp.float32) * inverse_permutation
    weight_factors = (jnp.exp(scores - group_totals[:, None]) - positive.T).astype(jnp.bfloat16)
    unit_p = jnp.dot(weight_factors.T, group_q, preferred_element_type=jnp.float32) * factor
    return_table = local_rows[:, None] == served_flat[None, :]
    own_terms = hard_w.astype(jnp.float32)[:, None] * qshort * factor
    term_slots = jnp.dot(
        slot_table.astype(jnp.float32),
        own_terms,
        precision=lax.Precision.HIGHEST,
        preferred_element_type=jnp.float32,
    )
    grad_terms = lax.all_to_all(
        term_slots.reshape(batch_count, capacity, embedding_dimension).astype(jnp.bfloat16),
        "batch",
        split_axis=0,
        concat_axis=0,
        tiled=True,
    ).astype(jnp.float32)
    spread = jnp.dot(
        return_table.astype(jnp.float32),
        grad_terms.reshape(slot_total, embedding_dimension),
        precision=lax.Precision.HIGHEST,
        preferred_element_type=jnp.float32,
    )
    passage_grad = norm_back(passages, pscale, unit_p + spread).astype(jnp.bfloat16)
    return (query_grad, passage_grad)


def solution(mesh):
    in_specs = (P(("batch", "grp"), None), P(("batch", "grp"), None), P(("batch", "grp")))
    out_specs = (P(("batch", "grp"), None), P(("batch", "grp"), None))
    return jax.shard_map(local, mesh=mesh, in_specs=in_specs, out_specs=out_specs, check_vma=False)
```

profile of v0, /device:TPU:1, one launch (start us, length us, event | category | flops | bytes accessed | tf_op | source)
XLA Modules:
  0.0 299.7 jit_solution(11215071971105043253)
XLA Ops:
  7.2 0.7 and_select_fusion.1
  8.1 0.8 all_to_all.12
  8.9 20.6 %all-to-all-start = ((s32[128,1,2]{2,1,0:T(1,128)}), s32[128,1,2]{2,1,0:T(1,128)S(1)}, u32[]{:S(2)}, u32[]{:S(2)}) async-start(s32[128,1,2]{2,1,0:T(1,128)} %bitcast), calls=%async_computation | async-start | bytes 131072 | tf_op jit(solution)/shard_map/all_to_all | solution.py:47
  29.5 1.5 fusion.9
  31.0 1.5 fusion.10
  32.5 11.8 %all-to-all-done = s32[128,1,2]{2,1,0:T(1,128)S(1)} async-done(((s32[128,1,2]{2,1,0:T(1,128)}), s32[128,1,2]{2,1,0:T(1,128)S(1)}, u32[]{:S(2)}, u32[]{:S(2)}) %all-to-all-start) | async-done | bytes 1056 | tf_op jit(solution)/shard_map/all_to_all | solution.py:47
  44.3 0.5 broadcast.164
  44.8 0.8 reduce.7
  45.8 1.8 gather_fusion
  47.7 2.7 gather.11
  50.4 5.0 %broadcast_select_fusion = bf16[128,2,4096]{2,1,0:T(2,128)(2,1)} fusion(bf16[128,2,4096]{2,1,0:T(2,128)(2,1)} %gather.11, pred[128,2]{1,0:T(8,128)(4,1)S(1)} %compare_and_fusion), kind=kLoop, calls=%fused_computation.6 | loop fusion | flops 1048576 | bytes 4194560 | tf_op jit(solution)/shard_map/jit(_take)/select_n | solution.py:49
  55.4 6.9 %all-to-all-start.1 = ((bf16[128,2,4096]{2,1,0:T(2,128)(2,1)}), bf16[128,2,4096]{2,1,0:T(2,128)(2,1)}, u32[]{:S(2)}, u32[]{:S(2)}) async-start(bf16[128,2,4096]{2,1,0:T(2,128)(2,1)} %broadcast_select_fusion), calls=%async_computation.1 | async-start | bytes 4194304 | tf_op jit(solution)/shard_map/all_to_all | solution.py:52
  62.5 0.5 all-gather.4.cloned.1.call-update
  63.1 0.3 fusion.3
  63.4 95.5 %all-to-all-done.1 = bf16[128,2,4096]{2,1,0:T(2,128)(2,1)} async-done(((bf16[128,2,4096]{2,1,0:T(2,128)(2,1)}), bf16[128,2,4096]{2,1,0:T(2,128)(2,1)}, u32[]{:S(2)}, u32[]{:S(2)}) %all-to-all-start.1) | async-done | bytes 2097184 | tf_op jit(solution)/shard_map/all_to_all | solution.py:52
  158.8 2.7 reshape.122
  161.6 2.2 gather_fusion.1
  163.8 1.8 fusion
  165.6 4.2 %exponential_reduce_fusion = (f32[128]{0:T(128)S(1)}, f32[128,512]{1,0:T(8,128)S(1)}) fusion(bf16[128,4096]{1,0:T(8,128)(2,1)S(1)} %get-tuple-element.7, bf16[512,4096]{1,0:T(8,128)(2,1)} %all-gather.4.cloned.1.call-done), kind=kOutput, calls=%fused_computation.45 | convolution fusion | flops 537001856 | bytes 5505536 | tf_op jit(solution)/shard_map/dot_general | solution.py:61
  169.8 3.4 %convolution_convert_fusion = bf16[256,4096]{1,0:T(8,128)(2,1)} fusion(bf16[128,4096]{1,0:T(8,128)(2,1)S(1)} %get-tuple-element.7, f32[128]{0:T(128)S(1)} %get-tuple-element.4, s32[128]{0:T(128)S(1)} %get-tuple-element.9), kind=kOutput, calls=%fused_computation.2 | convolution fusion | flops 1613266944 | bytes 3146752 | tf_op jit(solution)/shard_map/dot_general | solution.py:81
  173.2 4.4 %convert_element_type.74 = bf16[128,2,4096]{2,1,0:T(2,128)(2,1)} reshape(bf16[256,4096]{1,0:T(8,128)(2,1)} %convolution_convert_fusion) | data formatting | bytes 4194304 | tf_op jit(solution)/shard_map/convert_element_type | solution.py:88
  177.6 10.8 %all-to-all-start.2 = ((bf16[128,2,4096]{2,1,0:T(2,128)(2,1)}), bf16[128,2,4096]{2,1,0:T(2,128)(2,1)}, u32[]{:S(2)}, u32[]{:S(2)}) async-start(bf16[128,2,4096]{2,1,0:T(2,128)(2,1)} %convert_element_type.74), calls=%async_computation.2 | async-start | bytes 4194304 | tf_op jit(solution)/shard_map/all_to_all | solution.py:87
  188.4 0.7 all-gather.6.cloned.1.call-update
  189.3 8.7 %all-gather = f32[4,1,128]{2,1,0:T(1,128)S(1)} all-gather(f32[1,1,128]{2,1,0:T(1,128)S(1)} %bitcast.17), channel_id=1, replica_groups=mesh['batch'=128,'grp'=4] {'grp'}, dimensions={0}, use_global_device_ids=true | all-gather | bytes 2560 | tf_op jit(solution)/shard_map/all_gather | solution.py:75
  198.0 3.5 %fusion.8 = (f32[128]{0:T(128)S(1)}, f32[128,4096]{1,0:T(8,128)S(1)}) fusion(bf16[128,4096]{1,0:T(8,128)(2,1)S(1)} %copy-done.4, bf16[128,4096]{1,0:T(8,128)(2,1)S(1)} %copy-done.5, pred[128]{0:T(512)(128)(4,1)S(1)} %get-tuple-element.8, f32[128]{0:T(128)S(1)} %get-tuple-element.4, bf16[512,4096]{1,0:T(8,128)(2,1)} %all-gather.4.cloned.1.call-done, ...), kind=kOutput, calls=%fused_computation.25 | convolution fusion | flops 541392768 | bytes 8652928 | tf_op jit(solution)/shard_map/dot_general | solution.py:71
  201.5 1.6 fusion.7
  203.1 45.0 %all-gather.6.cloned.1.call-done = bf16[512,4096]{1,0:T(8,128)(2,1)} async-done(((bf16[128,4096]{1,0:T(8,128)(2,1)}), bf16[512,4096]{1,0:T(8,128)(2,1)}) %all-gather.6.cloned.1.call-update) | async-done | bytes 4194320 | tf_op jit(solution)/shard_map/all_gather | solution.py:56
  248.1 6.4 %convolution_multiply_fusion = f32[128,4096]{1,0:T(8,128)S(1)} fusion(bf16[512,4096]{1,0:T(8,128)(2,1)} %all-gather.6.cloned.1.call-done, bf16[128,4096]{1,0:T(8,128)(2,1)S(1)} %copy-done.1, s32[128]{0:T(128)S(1)} %iota_add_fusion, f32[512]{0:T(512)S(1)} %bitcast.15), kind=kOutput, calls=%fused_computation.4 | convolution fusion | flops 1074659328 | bytes 7342592 | tf_op jit(solution)/shard_map/dot_general | solution.py:78
  254.6 30.3 %all-to-all-done.2 = bf16[128,2,4096]{2,1,0:T(2,128)(2,1)} async-done(((bf16[128,2,4096]{2,1,0:T(2,128)(2,1)}), bf16[128,2,4096]{2,1,0:T(2,128)(2,1)}, u32[]{:S(2)}, u32[]{:S(2)}) %all-to-all-start.2) | async-done | bytes 2097184 | tf_op jit(solution)/shard_map/all_to_all | solution.py:87
  284.9 4.1 %reshape.124 = bf16[256,4096]{1,0:T(8,128)(2,1)} reshape(bf16[128,2,4096]{2,1,0:T(2,128)(2,1)} %all-to-all-done.2) | data formatting | bytes 4194304 | tf_op jit(solution)/shard_map/reshape | solution.py:96
  289.0 2.2 fusion.14
  291.2 1.6 fusion.13
  (32 shorter events, 1.0 us)
Async XLA Ops:
  8.9 35.4 %all-to-all-start = ((s32[128,1,2]{2,1,0:T(1,128)}), s32[128,1,2]{2,1,0:T(1,128)S(1)}, u32[]{:S(2)}, u32[]{:S(2)}) async-start(s32[128,1,2]{2,1,0:T(1,128)} %bitcast), calls=%async_computation | async-start | bytes 131072 | tf_op jit(solution)/shard_map/all_to_all | solution.py:47
  32.5 15.1 %copy-start = (bf16[128,4096]{1,0:T(8,128)(2,1)}, bf16[128,4096]{1,0:T(8,128)(2,1)S(1)}, u32[]{:S(2)}) copy-start(bf16[128,4096]{1,0:T(8,128)(2,1)S(1)} %fusion.10) | copy-start | bytes 3145732
  55.4 7.7 %copy-start.4 = (bf16[128,4096]{1,0:T(8,128)(2,1)S(1)}, bf16[128,4096]{1,0:T(8,128)(2,1)}, u32[]{:S(2)}) copy-start(bf16[128,4096]{1,0:T(8,128)(2,1)} %param.3) | copy-start | bytes 3145732
  55.4 103.4 %all-to-all-start.1 = ((bf16[128,2,4096]{2,1,0:T(2,128)(2,1)}), bf16[128,2,4096]{2,1,0:T(2,128)(2,1)}, u32[]{:S(2)}, u32[]{:S(2)}) async-start(bf16[128,2,4096]{2,1,0:T(2,128)(2,1)} %broadcast_select_fusion), calls=%async_computation.1 | async-start | bytes 4194304 | tf_op jit(solution)/shard_map/all_to_all | solution.py:52
  62.3 103.3 %all-gather.4.cloned.1.call-start = ((), (), s32[]{:S(2)}) async-start(), calls=%async_computation.3 | async-start | bytes 5242880 | tf_op jit(solution)/shard_map/all_gather | solution.py:55
  165.6 4.2 %copy-start.3 = (bf16[128,4096]{1,0:T(8,128)(2,1)}, bf16[128,4096]{1,0:T(8,128)(2,1)S(1)}, u32[]{:S(2)}) copy-start(bf16[128,4096]{1,0:T(8,128)(2,1)S(1)} %get-tuple-element.7) | copy-start | bytes 3145732
  177.6 20.4 %copy-start.5 = (bf16[128,4096]{1,0:T(8,128)(2,1)S(1)}, bf16[128,4096]{1,0:T(8,128)(2,1)}, u32[]{:S(2)}) copy-start(bf16[128,4096]{1,0:T(8,128)(2,1)} %gather_fusion.1) | copy-start | bytes 3145732
  177.6 107.3 %all-to-all-start.2 = ((bf16[128,2,4096]{2,1,0:T(2,128)(2,1)}), bf16[128,2,4096]{2,1,0:T(2,128)(2,1)}, u32[]{:S(2)}, u32[]{:S(2)}) async-start(bf16[128,2,4096]{2,1,0:T(2,128)(2,1)} %convert_element_type.74), calls=%async_computation.2 | async-start | bytes 4194304 | tf_op jit(solution)/shard_map/all_to_all | solution.py:87
  188.4 59.7 %all-gather.6.cloned.1.call-start = ((), (), s32[]{:S(2)}) async-start(), calls=%async_computation.4 | async-start | bytes 5242880 | tf_op jit(solution)/shard_map/all_gather | solution.py:56
  201.5 46.6 %copy-start.1 = (bf16[128,4096]{1,0:T(8,128)(2,1)S(1)}, bf16[128,4096]{1,0:T(8,128)(2,1)}, u32[]{:S(2)}) copy-start(bf16[128,4096]{1,0:T(8,128)(2,1)} %copy-done) | copy-start | bytes 3145732
  254.6 34.4 %copy-start.2 = (bf16[128,4096]{1,0:T(8,128)(2,1)S(1)}, bf16[128,4096]{1,0:T(8,128)(2,1)}, u32[]{:S(2)}) copy-start(bf16[128,4096]{1,0:T(8,128)(2,1)} %param.4) | copy-start | bytes 3145732
Sparse Core Ops, SparseCore 0:
  65.2 56.8 all-gather.3
  191.3 56.7 all-gather.5
where the time goes:
time: 302 us; the launch traced here: 300 us
  waiting for transfers between devices  184 us (61%)
  starting transfers between devices  38.5 us (13%)
  matrix products  19.7 us (7%)
  local copies, waits for them, and re-layouts  19.6 us (6%)
  other arithmetic  15.2 us (5%)
  between operations  14.2 us (5%)
  blocking collectives  8.67 us (3%)
    all_to_all x1, waiting for transfers between devices, local(): lax.all_to_all(served, 'batch', split_axis=0, concat_axis=0, tiled=True)  95.5 us
    all_gather x1, waiting for transfers between devices, local(): lax.all_gather(qshort, 'grp', axis=0, tiled=True)  45 us
    all_to_all x1, waiting for transfers between devices, local(): lax.all_to_all(term_slots.reshape(batch_count, capacity, embedding_dimens...  30.3 us
    all_to_all x1, starting transfers between devices, local(): lax.all_to_all(requests, 'batch', split_axis=0, concat_axis=0, tiled=True)  20.6 us
    all_to_all x1, waiting for transfers between devices, local(): lax.all_to_all(requests, 'batch', split_axis=0, concat_axis=0, tiled=True)  11.8 us
    all_to_all x1, starting transfers between devices, local(): lax.all_to_all(term_slots.reshape(batch_count, capacity, embedding_dimens...  10.8 us
    all_gather x1, blocking collectives, local(): group_totals = lax.all_gather(totals, 'grp', axis=0, tiled=True)  8.67 us
    all_to_all x1, starting transfers between devices, local(): lax.all_to_all(served, 'batch', split_axis=0, concat_axis=0, tiled=True)  6.9 us
  transfers between devices with their start and end apart: 5, of which 4 were waited for; matrix products, arithmetic and copies ran while one was open for 7% of the time, Pallas kernels for 0%

commit v1 on v0

v1 whole, which is shorter than its diff:
```python
import functools

import jax
import jax.numpy as jnp
from jax import lax
from jax.experimental import pallas as pl
from jax.experimental.pallas import tpu as pltpu
from jax.sharding import PartitionSpec as P

SOFTMAX_TEMPER = 0.02
LOSS_SCALE = 64.0
EPSILON = 1e-06

PLANES = 16
PLANE = 8
FAR = PLANES // 2
SLOTS = 2
OWN = PLANE * SLOTS
CAPS = [0, 84, 76, 68, 60, 50, 38, 24, 8, 0]
LANES = 128


def row_scales(values):
    floats = values.astype(jnp.float32)
    return lax.rsqrt(jnp.mean(floats * floats, -1, keepdims=True) + EPSILON)


def norm_back(values, scales, upstream):
    floats = values.astype(jnp.float32)
    return scales * upstream - scales * scales * scales * floats * jnp.mean(
        floats * upstream, -1, keepdims=True
    )


def offsets_of(sizes):
    out, total = [], 0
    for size in sizes:
        out.append(total)
        total += size
    return out, total


OUT_AT, OUT_ROWS = offsets_of([0] + [CAPS[d] for d in range(1, FAR + 1)])
CAP1 = CAPS[1]


def exchange_kernel(
    inv, srv, mrg, pick, fin,
    q3, p3, qs, ps,
    hard, owed, gp, gq,
    out, final, qfirst, pstage, qstage,
    own_sem, x_send, x_recv, qz_send, qz_recv, pz_send, pz_recv,
    py_send, py_recv, qy_send, qy_recv, *arriving
):
    comb = [[None, *arriving[s * FAR : (s + 1) * FAR]] for s in range(2)]
    qin = [[None, *arriving[(2 + s) * FAR : (3 + s) * FAR]] for s in range(2)]
    rows = q3.shape[0]
    half = rows // 2
    b = lax.axis_index("batch")
    g = lax.axis_index("grp")
    n_grp = 4
    z, me = b // PLANE, b % PLANE

    def plane(step):
        return lax.rem(z + step + PLANES, PLANES)

    def peer(j):
        return lax.rem(me + j, PLANE)

    ahead = [{"batch": plane(1) * PLANE + me}, {"batch": plane(-1) * PLANE + me}]
    right, left = lax.rem(g + 1, n_grp), lax.rem(g + n_grp - 1, n_grp)
    sides = [{"grp": right}, {"grp": left}]
    peers = [{"batch": z * PLANE + peer(j)} for j in range(1, PLANE)]

    barrier = pltpu.get_barrier_semaphore()
    greeted = ahead + sides + peers
    for device in greeted:
        pl.semaphore_signal(barrier, inc=1, device_id=device, device_id_type=pl.DeviceIdType.MESH)
    pl.semaphore_wait(barrier, len(greeted))

    def remote(src, dst, send, recv, device):
        return pltpu.make_async_remote_copy(
            src_ref=src, dst_ref=dst, send_sem=send, recv_sem=recv,
            device_id=device, device_id_type=pl.DeviceIdType.MESH,
        )

    def block(ref, who, start=0, size=rows):
        return ref.at[pl.ds(pl.multiple_of(who * rows + start, half), size), :]

    whole = ((ps, gp), (qs, gq))
    locals_ = []
    for a, (src, dst) in enumerate(whole):
        copy = pltpu.make_async_copy(src, block(dst, g), own_sem.at[a])
        copy.start()
        locals_.append(copy)
        for s in range(2):
            remote(src, block(dst, g), x_send.at[a, s], x_recv.at[a, s], sides[s]).start()

    def pass_on(a):
        dst = whole[a][1]
        for s, origin in ((0, left), (1, right)):
            remote(ps, block(dst, origin), x_send.at[a, s], x_recv.at[a, s], sides[s]).wait_recv()
            part = block(dst, origin, s * half, half)
            remote(part, part, x_send.at[a, 2 + s], x_recv.at[a, 2 + s], sides[s]).start()

    def x_end(a):
        dst = whole[a][1]
        across = lax.rem(g + 2, n_grp)
        for s in range(2):
            part = block(dst, across, s * half, half)
            remote(part, part, x_send.at[a, 2 + s], x_recv.at[a, 2 + s], sides[s]).wait()
            remote(ps, block(dst, g), x_send.at[a, s], x_recv.at[a, s], sides[s]).wait_send()

    def copy_rows(n, store, load):
        def body(r, carry):
            store(r, load(r))
            return carry

        lax.fori_loop(0, n, body, 0, unroll=False)

    def q_hop(s, d):
        if d == 1:
            src = qfirst.at[s]
        else:
            src = qin[s][d - 1].at[pl.ds(0, CAPS[d])]
        return remote(
            src, qin[s][d], qz_send.at[s, d], qz_recv.at[s, d], ahead[1 - s]
        )

    for s in range(2):
        def store(r, value, s=s):
            qfirst[s, r] = value

        def load(r, s=s):
            return q3[inv[s, r]]

        copy_rows(CAP1, store, load)
        q_hop(s, 1).start()

    def p_owed(s, d):
        return plane(d) if s == 0 else plane(-d)

    def partners(s, d):
        return range(s, PLANE, 2) if d == FAR else range(PLANE)

    def p_spread(s, d):
        target = p_owed(s, d)
        place = pl.ds(me * SLOTS, SLOTS)
        others = 0
        for j in partners(s, d):
            for k in range(SLOTS):
                row = p3[srv[target * PLANE + peer(j), k]]
                if j == 0:
                    comb[s][d][me * SLOTS + k] = row
                else:
                    pstage[s, d, others * SLOTS + k] = row
            if j:
                others += 1
        others = 0
        for j in partners(s, d):
            if j:
                remote(
                    pstage.at[s, d, pl.ds(others * SLOTS, SLOTS)], comb[s][d].at[place],
                    py_send.at[s, d], py_recv.at[s, d], peers[j - 1],
                ).start()
                others += 1

    def p_spread_near():
        near = 2 * CAP1
        for k in range(SLOTS):
            final[near + me * SLOTS + k] = p3[srv[z * PLANE + me, k]]
        for j in range(1, PLANE):
            for k in range(SLOTS):
                pstage[0, 0, (j - 1) * SLOTS + k] = p3[srv[z * PLANE + peer(j), k]]
        for j in range(1, PLANE):
            remote(
                pstage.at[0, 0, pl.ds((j - 1) * SLOTS, SLOTS)],
                final.at[pl.ds(near + me * SLOTS, SLOTS)],
                py_send.at[0, 0], py_recv.at[0, 0], peers[j - 1],
            ).start()

    def spread_bytes(s, d):
        n = SLOTS * len([j for j in partners(s, d) if j])
        return pstage.at[s, d, pl.ds(0, n)]

    for d in range(FAR, 0, -1):
        for s in range(2):
            p_spread(s, d)
    p_spread_near()

    def p_hop(s, d):
        src = out.at[s, pl.ds(OUT_AT[d], CAPS[d])]
        if d == 1:
            dst = final.at[pl.ds(s * CAP1, CAP1)]
        else:
            dst = comb[s][d - 1].at[pl.ds(OWN, CAPS[d])]
        return remote(src, dst, pz_send.at[s, d], pz_recv.at[s, d], ahead[s])

    def p_step(s, d):
        here = spread_bytes(s, d)
        pltpu.make_async_copy(here, here, py_recv.at[s, d]).wait()
        if d < FAR:
            p_hop(s, d + 1).wait_recv()
        target = p_owed(s, d)

        def store(r, value):
            out[s, OUT_AT[d] + r] = value

        def load(r):
            return comb[s][d][mrg[target, s, r]]

        copy_rows(CAPS[d], store, load)
        p_hop(s, d).start()

    def q_spread(s, d):
        source = plane(d) if s == 0 else plane(-d)

        def take(j, k):
            at = pick[source, peer(j) * SLOTS + k]
            if d == 0:
                return q3[at]
            return qin[j % 2 if d == FAR else s][d][at]

        place = (source * PLANE + me) * SLOTS
        line = 2 * d + s
        for j in range(PLANE):
            for k in range(SLOTS):
                qstage[line, j * SLOTS + k] = take(j, k)
        pltpu.make_async_copy(
            qstage.at[line, pl.ds(0, SLOTS)], owed.at[pl.ds(place, SLOTS)], own_sem.at[2 + line]
        ).start()
        for j in range(1, PLANE):
            remote(
                qstage.at[line, pl.ds(j * SLOTS, SLOTS)], owed.at[pl.ds(place, SLOTS)],
                qy_send.at[line], qy_recv.at[line], peers[j - 1],
            ).start()

    q_spread(0, 0)
    for step in range(1, FAR + 1):
        for s in range(2):
            q_hop(s, step).wait_recv()
            if step < FAR:
                q_hop(s, step + 1).start()
        for s in range(2):
            p_step(s, FAR + 1 - step)
        for s in range(2):
            if step < FAR or s == 0:
                q_spread(s, step)
        if step == 2:
            pass_on(0)
        if step == 4:
            pass_on(1)

    for s in range(2):
        p_hop(s, 1).wait_recv()
    here = spread_bytes(0, 0)
    pltpu.make_async_copy(here, here, py_recv.at[0, 0]).wait()

    def store(r, value):
        hard[r] = value

    def load(r):
        return final[fin[r]]

    copy_rows(rows, store, load)

    x_end(0)
    x_end(1)
    for copy in locals_:
        copy.wait()
    for d in range(FAR + 1):
        for s in range(2):
            if (d == 0 or d == FAR) and s == 1:
                continue
            line = 2 * d + s
            sent = qstage.at[line, pl.ds(SLOTS, OWN - SLOTS)]
            pltpu.make_async_copy(sent, sent, qy_send.at[line]).wait()
            pltpu.make_async_copy(sent, sent, qy_recv.at[line]).wait()
            pltpu.make_async_copy(
                qstage.at[line, pl.ds(0, SLOTS)], owed.at[pl.ds(0, SLOTS)], own_sem.at[2 + line]
            ).wait()
    for d in range(FAR + 1):
        for s in range(2):
            if d == 0 and s == 1:
                continue
            here = spread_bytes(s, d)
            pltpu.make_async_copy(here, here, py_send.at[s, d]).wait()
            if d > 0:
                q_hop(s, d).wait_send()
                p_hop(s, d).wait_send()


def exchange(inv, srv, mrg, pick, fin, q3, p3, qs, ps):
    rows, width = qs.shape
    line = (width // LANES, LANES)
    slot_total = PLANES * PLANE * SLOTS
    smem = pl.BlockSpec(memory_space=pltpu.SMEM)
    vmem = pl.BlockSpec(memory_space=pltpu.VMEM)
    hbm = pl.BlockSpec(memory_space=pl.ANY)
    dma = pltpu.SemaphoreType.DMA

    def buffer(*lead):
        return pltpu.VMEM(lead + line, jnp.bfloat16)

    return pl.pallas_call(
        exchange_kernel,
        out_shape=(
            jax.ShapeDtypeStruct((rows,) + line, jnp.bfloat16),
            jax.ShapeDtypeStruct((slot_total,) + line, jnp.bfloat16),
            jax.ShapeDtypeStruct((4 * rows, width), jnp.bfloat16),
            jax.ShapeDtypeStruct((4 * rows, width), jnp.bfloat16),
        ),
        in_specs=[smem] * 5 + [vmem, vmem, hbm, hbm],
        out_specs=(vmem, vmem, hbm, hbm),
        scratch_shapes=[
            buffer(2, OUT_ROWS),
            buffer(2 * CAP1 + OWN),
            buffer(2, CAP1),
            buffer(2, FAR + 1, OWN),
            buffer(2 * (FAR + 1), OWN),
            dma((2 + 2 * (FAR + 1),)),
            dma((2, 4)), dma((2, 4)),
            dma((2, FAR + 1)), dma((2, FAR + 1)),
            dma((2, FAR + 1)), dma((2, FAR + 1)),
            dma((2, FAR + 1)), dma((2, FAR + 1)),
            dma((2 * (FAR + 1),)), dma((2 * (FAR + 1),)),
            *[buffer(OWN + CAPS[d + 1]) for _ in range(2) for d in range(1, FAR + 1)],
            *[buffer(CAPS[d]) for _ in range(2) for d in range(1, FAR + 1)],
        ],
        compiler_params=pltpu.CompilerParams(
            collective_id=0, has_side_effects=True, vmem_limit_bytes=60 * 1024 * 1024
        ),
        cost_estimate=pl.CostEstimate(flops=0, bytes_accessed=40 * 1024 * 1024, transcendentals=0),
        name="exchange",
    )(inv, srv, mrg, pick, fin, q3, p3, qs, ps)


def column_kernel(x, full, here, plane_send, plane_recv, z_send, z_recv):
    b = lax.axis_index("batch")
    z, me = b // PLANE, b % PLANE
    peers = [{"batch": z * PLANE + lax.rem(me + j, PLANE)} for j in range(1, PLANE)]
    lines = [{"batch": lax.rem(z + j, PLANES) * PLANE + me} for j in range(1, PLANES)]
    barrier = pltpu.get_barrier_semaphore()
    for device in peers + lines:
        pl.semaphore_signal(barrier, inc=1, device_id=device, device_id_type=pl.DeviceIdType.MESH)
    pl.semaphore_wait(barrier, len(peers + lines))

    def send(src, dst, sems, device):
        pltpu.make_async_remote_copy(
            src_ref=src, dst_ref=dst, send_sem=sems[0].at[0], recv_sem=sems[1].at[0],
            device_id=device, device_id_type=pl.DeviceIdType.MESH,
        ).start()

    def settle(rows, sem):
        ref = full.at[pl.ds(0, rows)]
        pltpu.make_async_copy(ref, ref, sem.at[0]).wait()

    full[b] = x[...]
    here[0] = x[...]
    for device in peers:
        send(here.at[0], full.at[b], (plane_send, plane_recv), device)
    settle(PLANE - 1, plane_recv)
    mine = full.at[pl.ds(z * PLANE, PLANE)]
    for device in lines:
        send(mine, mine, (z_send, z_recv), device)
    settle(PLANE * (PLANES - 1), z_recv)
    settle(PLANE - 1, plane_send)
    settle(PLANE * (PLANES - 1), z_send)


def column(x, collective_id, name):
    rows = x.shape[0]
    dma = pltpu.SemaphoreType.DMA((1,))
    full = pl.pallas_call(
        column_kernel,
        out_shape=jax.ShapeDtypeStruct((PLANES * PLANE, 1, rows), x.dtype),
        in_specs=[pl.BlockSpec(memory_space=pltpu.VMEM)],
        out_specs=pl.BlockSpec(memory_space=pltpu.VMEM),
        scratch_shapes=[pltpu.VMEM((1, 1, rows), x.dtype), dma, dma, dma, dma],
        compiler_params=pltpu.CompilerParams(collective_id=collective_id, has_side_effects=True),
        name=name,
    )(x.reshape(1, rows))
    return full.reshape(PLANES * PLANE, rows)


def course(ahead, owner_me, me):
    tie = (owner_me + me) % 2
    side = jnp.where(ahead == 0, 2, jnp.where(ahead < FAR, 0, jnp.where(ahead == FAR, tie, 1)))
    return side, jnp.where(ahead <= FAR, ahead, PLANES - ahead)


def too_many(ids_all, rows):
    who = jnp.arange(PLANES * PLANE)
    owner = ids_all // rows
    ahead = (who[:, None] // PLANE - owner // PLANE + PLANES) % PLANES
    side, dist = course(ahead, owner % PLANE, (who % PLANE)[:, None])
    hops = jnp.arange(2 * FAR)
    caps = jnp.zeros((2 * FAR,), jnp.int32)
    for d in range(1, FAR + 1):
        caps = jnp.where(hops % FAR == d - 1, CAPS[d], caps)
    uses = (side[:, None, :] == hops[None, :, None] // FAR) & (dist[:, None, :] > hops[None, :, None] % FAR)
    need = jnp.sum(uses.astype(jnp.int32), 2)
    return jnp.max(jnp.where(need > caps[None, :], 1, 0)) > 0


def tables(ids_all, b, rows):
    z, me = b // PLANE, b % PLANE
    r = jnp.arange(rows)
    planes = jnp.arange(PLANES)
    line = lax.dynamic_slice_in_dim(ids_all.reshape(PLANES, PLANE, rows), me, 1, 1)[:, 0]
    owner = line // rows
    oz, om = owner // PLANE, owner % PLANE
    earlier = r[None, :] < r[:, None]
    slot = jnp.sum(((owner[:, :, None] == owner[:, None, :]) & earlier).astype(jnp.int32), 2)
    ahead = (planes[:, None] - oz + PLANES) % PLANES
    side, dist = course(ahead, om, me)
    key = dist * rows + (rows - 1 - r)[None, :]
    before = (side[:, :, None] == side[:, None, :]) & (key[:, None, :] > key[:, :, None])
    pos = jnp.sum(before.astype(jnp.int32), 2)
    cell = om * SLOTS + slot
    mine = oz == z

    at = jnp.arange(CAP1)
    sides = jnp.arange(2)
    hit = (side[:, None, None, :] == sides[None, :, None, None]) & (
        pos[:, None, None, :] == at[None, None, :, None]
    )
    placed = jnp.max(jnp.where(hit & mine[:, None, None, :], cell[:, None, None, :], -1), 3)
    far = jnp.stack([(planes - z + PLANES) % PLANES, (z - planes + PLANES) % PLANES], 1)
    room = jnp.zeros_like(far)
    for d in range(1, FAR):
        room = jnp.where(far == d, CAPS[d + 1], room)
    filler = SLOTS * ((me + sides) % PLANE)
    other = jnp.where(at[None, None, :] < room[:, :, None], OWN + at[None, None, :], filler[None, :, None])
    mrg = jnp.where(placed >= 0, placed, other)

    cells = jnp.arange(OWN)
    place = jnp.where(side == 2, r[None, :], pos)
    pick = jnp.sum(
        jnp.where(mine[:, None, :] & (cell[:, None, :] == cells[None, :, None]), place[:, None, :], 0), 2
    )

    def own(values):
        return lax.dynamic_slice_in_dim(values, z, 1, 0)[0]

    my_side, my_pos, my_cell = own(side), own(pos), own(cell)
    inv = jnp.sum(
        jnp.where(
            (my_side[None, None, :] == sides[:, None, None]) & (my_pos[None, None, :] == at[None, :, None]),
            r[None, None, :], 0,
        ), 2,
    )
    fin = jnp.where(my_side == 2, 2 * CAP1 + my_cell, my_side * CAP1 + my_pos)

    wanted = ids_all // rows == b
    code = r[None, :] * rows + ids_all % rows
    count = jnp.sum(wanted.astype(jnp.int32), 1)
    first = jnp.min(jnp.where(wanted, code, rows * rows), 1)
    last = jnp.max(jnp.where(wanted, code, 0), 1)
    first = jnp.where(count > 0, first, 0)
    codes = jnp.stack([first, last], 1)
    used = jnp.stack([count > 0, count > 1], 1)
    return inv, codes % rows, mrg, pick, fin, codes // rows, used, own(owner) * SLOTS + own(slot)


def padded(qshort, pshort, srv, home):
    rows, width = qshort.shape
    count = PLANES * PLANE

    def swap(values):
        moved = lax.all_to_all(
            values.reshape(count, SLOTS, width), "batch", split_axis=0, concat_axis=0, tiled=True
        )
        return moved.reshape(count * SLOTS, width)

    hard = jnp.take(swap(jnp.take(pshort, srv.reshape(-1), axis=0)), home, axis=0)
    sender = jnp.sum(
        jnp.where(jnp.arange(count * SLOTS)[:, None] == home[None, :], jnp.arange(rows)[None, :], 0), 1
    )
    return hard, swap(jnp.take(qshort, sender, axis=0))


def local(queries, passages, hard_ids):
    pair_rows, embedding_dimension = queries.shape
    batch_count = lax.axis_size("batch")
    group_rows = lax.axis_size("grp") * pair_rows
    group_pos = lax.axis_index("grp")
    scale = 1.0 / (embedding_dimension * SOFTMAX_TEMPER)
    factor = LOSS_SCALE * scale
    line = (pair_rows, embedding_dimension // LANES, LANES)

    ids_all = column(hard_ids, 1, "hard_ids_column")
    qscale = row_scales(queries)
    pscale = row_scales(passages)
    qshort = (queries.astype(jnp.float32) * qscale).astype(jnp.bfloat16)
    pshort = (passages.astype(jnp.float32) * pscale).astype(jnp.bfloat16)
    inv, srv, mrg, pick, fin, asker_row, used, home = tables(ids_all, lax.axis_index("batch"), pair_rows)
    hard3, owed3, group_p, group_q = exchange(
        inv, srv, mrg, pick, fin, qshort.reshape(line), pshort.reshape(line), qshort, pshort
    )
    hard_p, owed = lax.cond(
        too_many(ids_all, pair_rows),
        lambda: padded(qshort, pshort, srv, home),
        lambda: (hard3.reshape(pair_rows, embedding_dimension), owed3.reshape(-1, embedding_dimension)),
    )

    local_rows = jnp.arange(pair_rows)
    own_cols = group_pos * pair_rows + local_rows
    positive = (jnp.arange(group_rows)[None, :] == own_cols[:, None]).astype(jnp.float32)
    inner_scores = jnp.dot(qshort, group_p.T, preferred_element_type=jnp.float32) * scale
    hard_score = jnp.sum(qshort.astype(jnp.float32) * hard_p.astype(jnp.float32), 1) * scale
    totals = jnp.log(jnp.sum(jnp.exp(inner_scores), 1) + jnp.exp(hard_score))
    hard_w = jnp.exp(hard_score - totals).astype(jnp.bfloat16)
    group_totals = lax.all_gather(totals, "grp", axis=0, tiled=True)
    weights_all = column(hard_w.astype(jnp.float32), 2, "weights_column")

    inner_w = (jnp.exp(inner_scores - totals[:, None]) - positive).astype(jnp.bfloat16)
    unit_q = (
        jnp.dot(inner_w, group_p, preferred_element_type=jnp.float32)
        + hard_w.astype(jnp.float32)[:, None] * hard_p
    ) * factor
    query_grad = norm_back(queries, qscale, unit_q).astype(jnp.bfloat16)

    asked = asker_row[:, :, None] == local_rows[None, None, :]
    slot_w = jnp.sum(jnp.where(asked & used[:, :, None], weights_all[:, None, :], 0.0), 2).reshape(-1)
    spread_w = jnp.where(local_rows[:, None] == srv.reshape(-1)[None, :], slot_w[None, :], 0.0)
    scores = jnp.dot(group_q, pshort.T, preferred_element_type=jnp.float32) * scale
    inner_t = (jnp.exp(scores - group_totals[:, None]) - positive.T).astype(jnp.bfloat16)
    unit_p = (
        jnp.dot(inner_t.T, group_q, preferred_element_type=jnp.float32)
        + jnp.dot(spread_w.astype(jnp.bfloat16), owed, preferred_element_type=jnp.float32)
    ) * factor
    passage_grad = norm_back(passages, pscale, unit_p).astype(jnp.bfloat16)
    return (query_grad, passage_grad)


def solution(mesh):
    in_specs = (P(("batch", "grp"), None), P(("batch", "grp"), None), P(("batch", "grp")))
    out_specs = (P(("batch", "grp"), None), P(("batch", "grp"), None))
    return jax.shard_map(local, mesh=mesh, in_specs=in_specs, out_specs=out_specs, check_vma=False)
```

time: 302 us -> 271 us (0.90)
  Pallas kernels: 0 us -> 204 us
  waiting for transfers between devices: 184 us -> 0 us
  starting transfers between devices: 38.5 us -> 0 us
  between operations: 14.2 us -> 1.67 us
  other arithmetic: 15.2 us -> 24.4 us
  local copies, waits for them, and re-layouts: 19.6 us -> 12.1 us
    pallas_call x0 -> x3, Pallas kernels: none -> 204 us  [the longest x1 154 us: exchange(): pl.pallas_call(exchange_kernel, out_shape=(jax.ShapeDtypeStruct((rows,) +...]
    all_to_all x3 -> x0, waiting for transfers between devices: 138 us -> none  [the longest x1 95.5 us: local(): lax.all_to_all(served, 'batch', split_axis=0, concat_axis=0, tiled=True)]
    all_gather x2 -> x0, waiting for transfers between devices: 45.1 us -> none  [the longest x1 45 us: local(): lax.all_gather(qshort, 'grp', axis=0, tiled=True)]
    all_to_all x3 -> x0, starting transfers between devices: 38.2 us -> none  [the longest x1 20.6 us: local(): lax.all_to_all(requests, 'batch', split_axis=0, concat_axis=0, tiled=True)]
    reduce_sum x2 -> x7, other arithmetic: 0.29 us -> 9.33 us  [the longest x1 2.3 us: too_many(): need = jnp.sum(uses.astype(jnp.int32), 2)]
    reshape x4 -> x0, local copies, waits for them, and re-layouts: 7.12 us -> none  [the longest x1 4.1 us: local(): grad_terms.reshape(slot_total, embedding_dimension)]
    gather x3 -> x0, local copies, waits for them, and re-layouts: 6.69 us -> none  [the longest x2 4.53 us: local(): jnp.take(pshort, served_flat, axis=0)]
    another operation x0 -> x7, local copies, waits for them, and re-layouts: none -> 6.15 us
  transfers between devices with their start and end apart: 5 -> 0, of which waited for: 4 -> 0; matrix products, arithmetic and copies ran while one was open for 7% -> 0% of each run, Pallas kernels for 0% -> 0%
where the time goes in v1:
time: 271 us; the launch traced here: 268 us
  Pallas kernels  204 us (75%)
  other arithmetic  24.4 us (9%)
  matrix products  17.8 us (7%)
  local copies, waits for them, and re-layouts  12.1 us (4%)
  blocking collectives  8.39 us (3%)
    pallas_call x1, Pallas kernels, exchange(): pl.pallas_call(exchange_kernel, out_shape=(jax.ShapeDtypeStruct((rows,) +...  154 us
    pallas_call x2, Pallas kernels, column(): pl.pallas_call(column_kernel, out_shape=jax.ShapeDtypeStruct((PLANES * PL...  49.8 us
    all_gather x1, blocking collectives, local(): group_totals = lax.all_gather(totals, 'grp', axis=0, tiled=True)  8.39 us
    dot_general x1, matrix products, local(): jnp.dot(inner_t.T, group_q, preferred_element_type=jnp.float32)  7.82 us
    another operation x5, local copies, waits for them, and re-layouts  5.9 us

profile of v1, /device:TPU:1, one launch (start us, length us, event | category | flops | bytes accessed | tf_op | source)
XLA Modules:
  0.0 268.4 jit_solution(14838043634836638592)
XLA Ops:
  0.7 26.4 %hard_ids_column.1 = s32[128,1,128]{2,1,0:T(1,128)} custom-call(s32[1,128]{1,0:T(1,128)} %bitcast.112), custom_call_target="tpu_custom_call" | custom-call | tf_op jit(solution)/shard_map/hard_ids_column/pallas_call | solution.py:374
  27.0 0.9 constant_dynamic-slice_fusion.3
  28.0 0.6 convert_reduce_fusion.1
  28.7 1.0 convert_reduce_fusion.2
  29.8 0.9 select_reduce_fusion.3.pick
  30.8 2.9 %select_reduce_fusion.1 = s32[16,2,84]{0,2,1:T(8,128)S(1)} fusion(s32[16,128]{1,0:T(8,128)S(1)} %get-tuple-element.90, pred[16,128]{1,0:T(8,128)(4,1)S(1)} %get-tuple-element.82, pred[16,84,128]{2,0,1:T(8,128)(4,1)S(1)} %iota_compare_fusion.1, pred[16,2,128]{2,0,1:T(8,128)(4,1)S(1)} %iota_compare_fusion.10), kind=kLoop, calls=%fused_computation.44 | loop fusion | flops 1373568 | bytes 197120 | tf_op jit(solution)/shard_map/reduce_max | solution.py:428
  33.9 0.7 compare_select_fusion.17.mrg
  35.2 1.5 fusion.25
  36.7 0.6 copy.46.inv
  37.3 1.0 select_reduce_fusion.5
  40.7 0.6 fusion.1
  41.3 1.2 copy.55
  42.5 1.2 copy.56
  43.7 154.2 %exchange.1 = (bf16[128,32,128]{2,1,0:T(8,128)(2,1)}, bf16[256,32,128]{2,1,0:T(8,128)(2,1)}, bf16[512,4096]{1,0:T(8,128)(2,1)}, bf16[512,4096]{1,0:T(8,128)(2,1)}) custom-call(s32[2,84]{1,0:T(2,128)} %copy.46.inv, s32[128,2]{1,0:T(8,128)S(1)} %get-tuple-element.85.srv, s32[16,2,84]{2,1,0:T(2,128)} %compare_select_fusion.17.mrg, ...), custom_call_target="tpu_custom_call" | custom-call | bytes 41943040 | tf_op jit(solution)/shard_map/exchange/pallas_call | solution.py:305
  198.4 1.6 compare_select_fusion.10
  200.6 2.3 convert_reduce_fusion
  203.0 1.4 select_reduce_fusion.6
  205.0 5.4 %conditional.3 = (bf16[256,4096]{1,0:T(8,128)(2,1)}, f32[128,4096]{1,0:T(8,128)}) conditional(s32[]{:T(128)} %convert_element_type.107, (bf16[256,32,128]{2,1,0:T(8,128)(2,1)}, bf16[128,32,128]{2,1,0:T(8,128)(2,1)}) %tuple.27, (s32[16,128]{1,0:T(8,128)S(1)}, s32[]{:T(128)}, s32[128]{0:T(128)}, s32[16,128]{1,0:T(8,128)S(1)}, ...), branch_computations={%region_13.14_spmd, %region_14.17_spmd} | conditional | flops 3252864 | bytes 51413872
  205.0 3.1 %copy.59 = f32[16,8,32,128]{3,1,2,0:T(8,128)} copy(bf16[16,8,32,128]{3,2,1,0:T(8,128)(2,1)} %bitcast.98) | data formatting | bytes 3145728 | tf_op jit(solution)/shard_map/conditional.1
  208.2 2.3 copy.60
  210.4 1.9 multiply_reduce_fusion
  212.3 3.8 %exponential_reduce_fusion = (f32[128]{0:T(128)S(1)}, f32[128,512]{1,0:T(8,128)S(1)}) fusion(bf16[128,4096]{1,0:T(8,128)(2,1)S(1)} %get-tuple-element.106.qs, bf16[512,4096]{1,0:T(8,128)(2,1)} %get-tuple-element.53), kind=kOutput, calls=%fused_computation.65 | convolution fusion | flops 537001856 | bytes 5505536 | tf_op jit(solution)/shard_map/dot_general | solution.py:510
  216.1 0.5 convert_convert_fusion.x
  216.7 23.4 %weights_column.1 = f32[128,1,128]{2,1,0:T(1,128)} custom-call(f32[1,128]{1,0:T(1,128)} %convert_convert_fusion.x), custom_call_target="tpu_custom_call" | custom-call | tf_op jit(solution)/shard_map/weights_column/pallas_call | solution.py:374
  240.2 1.1 select_reduce_fusion.2
  241.6 8.4 %all-gather = f32[4,1,128]{2,1,0:T(1,128)S(1)} all-gather(f32[1,1,128]{2,1,0:T(1,128)S(1)} %bitcast.110), channel_id=1, replica_groups=mesh['batch'=128,'grp'=4] {'grp'}, dimensions={0}, use_global_device_ids=true | all-gather | bytes 2560 | tf_op jit(solution)/shard_map/all_gather | solution.py:514
  250.0 7.8 %fusion.16 = f32[128,4096]{1,0:T(8,128)} fusion(bf16[512,4096]{1,0:T(8,128)(2,1)} %get-tuple-element.57, bf16[128,4096]{1,0:T(8,128)(2,1)S(1)} %get-tuple-element.107.ps, s32[128]{0:T(128)S(1)} %iota_add_fusion, f32[512]{0:T(512)S(1)} %bitcast.109), kind=kOutput, calls=%fused_computation.51 | convolution fusion | flops 1074135040 | bytes 7342592 | tf_op jit(solution)/shard_map/dot_general | solution.py:530
  258.0 3.1 %fusion.11 = (f32[128]{0:T(128)S(1)}, f32[128,4096]{1,0:T(8,128)S(1)}) fusion(bf16[128,4096]{1,0:T(8,128)(2,1)S(1)} %copy-done, f32[128,4096]{1,0:T(8,128)} %fusion.16, bf16[256,4096]{1,0:T(8,128)(2,1)} %get-tuple-element.58, bf16[256]{0:T(256)(128)(2,1)S(1)} %broadcast_in_dim.288, s32[256]{0:T(256)S(1)} %and_select_fusion.6), kind=kOutput, calls=%fused_computation.42 | convolution fusion | flops 271122304 | bytes 7342080 | tf_op jit(solution)/shard_map/dot_general | solution.py:531
  261.1 1.6 fusion.10
  262.7 1.0 copy-done.1
  263.7 3.1 %fusion.5 = (f32[128]{0:T(128)S(1)}, f32[128,4096]{1,0:T(8,128)S(1)}) fusion(bf16[128,4096]{1,0:T(8,128)(2,1)S(1)} %copy-done.4, f32[128,4096]{1,0:T(8,128)} %get-tuple-element.59, f32[128]{0:T(128)S(1)} %get-tuple-element.76, bf16[512,4096]{1,0:T(8,128)(2,1)S(1)} %copy-done.1, f32[128,512]{1,0:T(8,128)S(1)} %get-tuple-element.95, ...), kind=kOutput, calls=%fused_computation.36 | convolution fusion | flops 540344192 | bytes 9701376 | tf_op jit(solution)/shard_map/dot_general | solution.py:519
  266.8 1.6 fusion.4
  (77 shorter events, 5.1 us)
Async XLA Ops:
  0.6 38.4 %copy-start = (bf16[128,4096]{1,0:T(8,128)(2,1)S(1)}, bf16[128,4096]{1,0:T(8,128)(2,1)}, u32[]{:S(2)}) copy-start(bf16[128,4096]{1,0:T(8,128)(2,1)} %param.8) | copy-start | bytes 3145732
  0.6 39.2 %copy-start.2 = (bf16[128,4096]{1,0:T(8,128)(2,1)S(1)}, bf16[128,4096]{1,0:T(8,128)(2,1)}, u32[]{:S(2)}) copy-start(bf16[128,4096]{1,0:T(8,128)(2,1)} %param.7) | copy-start | bytes 3145732
  38.3 0.6 copy-start.13
  39.0 1.7 copy-start.3
  39.9 1.4 copy-start.11
  40.7 0.6 copy-start.8
  43.7 154.7 %copy-start.6 = (s32[128,1,128]{2,1,0:T(1,128)S(1)}, s32[128,1,128]{2,1,0:T(1,128)}, u32[]{:S(2)}) copy-start(s32[128,1,128]{2,1,0:T(1,128)} %hard_ids_column.1) | copy-start | bytes 196612
  205.0 3.1 %copy-start.5 = (bf16[256,32,128]{2,1,0:T(8,128)(2,1)S(1)}, bf16[256,32,128]{2,1,0:T(8,128)(2,1)}, u32[]{:S(2)}) copy-start(bf16[256,32,128]{2,1,0:T(8,128)(2,1)} %get-tuple-element.36) | copy-start | bytes 6291460 | tf_op jit(solution)/shard_map/conditional.1
  212.3 27.9 %copy-start.14 = (s32[128]{0:T(128)S(1)}, s32[128]{0:T(128)}, u32[]{:S(2)}) copy-start(s32[128]{0:T(128)} %copy-done.13) | copy-start | bytes 1540
  258.0 3.1 %copy-start.12 = (f32[128]{0:T(128)S(1)}, f32[128]{0:T(128)}, u32[]{:S(2)}) copy-start(f32[128]{0:T(128)} %copy-done.11) | copy-start | bytes 1540
  258.0 3.1 %copy-start.10 = (f32[128]{0:T(128)S(1)}, f32[128]{0:T(128)}, u32[]{:S(2)}) copy-start(f32[128]{0:T(128)} %get-tuple-element.72) | copy-start | bytes 1540
  258.0 4.7 %copy-start.4 = (bf16[128,4096]{1,0:T(8,128)(2,1)S(1)}, bf16[128,4096]{1,0:T(8,128)(2,1)}, u32[]{:S(2)}) copy-start(bf16[128,4096]{1,0:T(8,128)(2,1)} %param.7) | copy-start | bytes 3145732
  261.1 2.6 copy-start.1
  263.7 3.1 %copy-start.9 = (f32[128]{0:T(128)S(1)}, f32[128]{0:T(128)}, u32[]{:S(2)}) copy-start(f32[128]{0:T(128)} %copy-done.8) | copy-start | bytes 1540
  263.7 3.2 %copy-start.7 = (f32[128]{0:T(128)S(1)}, f32[128]{0:T(128)}, u32[]{:S(2)}) copy-start(f32[128]{0:T(128)} %get-tuple-element.74) | copy-start | bytes 1540

commit v2 on v1

--- a/solution.py
+++ b/solution.py
@@ -18,6 +18,7 @@
 OWN = PLANE * SLOTS
 CAPS = [0, 84, 76, 68, 60, 50, 38, 24, 8, 0]
 LANES = 128
+LAG = 2
 
 
 def row_scales(values):
@@ -46,11 +47,12 @@
 
 def exchange_kernel(
     inv, srv, mrg, pick, fin,
-    q3, p3, qs, ps,
-    hard, owed, gp, gq,
-    out, final, qfirst, pstage, qstage,
+    q3, p3, qs, ps, queries, passages, qscale, pscale, asked, flag,
+    query_grad, passage_grad, flags,
+    gp, gq, out, final, qfirst, pstage, qstage, owed, floats, unit, scores, scores_t,
+    ends, gathered, weights, sums,
     own_sem, x_send, x_recv, qz_send, qz_recv, pz_send, pz_recv,
-    py_send, py_recv, qy_send, qy_recv, *arriving
+    py_send, py_recv, qy_send, qy_recv, t_send, t_recv, c_send, c_recv, *arriving
 ):
     comb = [[None, *arriving[s * FAR : (s + 1) * FAR]] for s in range(2)]
     qin = [[None, *arriving[(2 + s) * FAR : (3 + s) * FAR]] for s in range(2)]
@@ -67,13 +69,16 @@
     def peer(j):
         return lax.rem(me + j, PLANE)
 
-    ahead = [{"batch": plane(1) * PLANE + me}, {"batch": plane(-1) * PLANE + me}]
+    lines = [{"batch": plane(j) * PLANE + me} for j in range(1, PLANES)]
+    ahead = [lines[0], lines[-1]]
     right, left = lax.rem(g + 1, n_grp), lax.rem(g + n_grp - 1, n_grp)
     sides = [{"grp": right}, {"grp": left}]
     peers = [{"batch": z * PLANE + peer(j)} for j in range(1, PLANE)]
 
     barrier = pltpu.get_barrier_semaphore()
-    greeted = ahead + sides + peers
+    across = lax.rem(g + 2, n_grp)
+    sides.append({"grp": across})
+    greeted = lines + sides + peers
     for device in greeted:
         pl.semaphore_signal(barrier, inc=1, device_id=device, device_id_type=pl.DeviceIdType.MESH)
     pl.semaphore_wait(barrier, len(greeted))
@@ -105,7 +110,6 @@
 
     def x_end(a):
         dst = whole[a][1]
-        across = lax.rem(g + 2, n_grp)
         for s in range(2):
             part = block(dst, across, s * half, half)
             remote(part, part, x_send.at[a, 2 + s], x_recv.at[a, 2 + s], sides[s]).wait()
@@ -221,35 +225,97 @@
                 return q3[at]
             return qin[j % 2 if d == FAR else s][d][at]
 
-        place = (source * PLANE + me) * SLOTS
+        place = owed.at[:, me, source]
         line = 2 * d + s
         for j in range(PLANE):
             for k in range(SLOTS):
                 qstage[line, j * SLOTS + k] = take(j, k)
         pltpu.make_async_copy(
-            qstage.at[line, pl.ds(0, SLOTS)], owed.at[pl.ds(place, SLOTS)], own_sem.at[2 + line]
+            qstage.at[line, pl.ds(0, SLOTS)], place, own_sem.at[2 + line]
         ).start()
         for j in range(1, PLANE):
             remote(
-                qstage.at[line, pl.ds(j * SLOTS, SLOTS)], owed.at[pl.ds(place, SLOTS)],
+                qstage.at[line, pl.ds(j * SLOTS, SLOTS)], place,
                 qy_send.at[line], qy_recv.at[line], peers[j - 1],
             ).start()
 
+    def q_step(d):
+        for s in range(2):
+            q_hop(s, d).wait_recv()
+            if d < FAR:
+                q_hop(s, d + 1).start()
+        for s in range(2):
+            if d < FAR or s == 0:
+                q_spread(s, d)
+
+    width = qs.shape[1]
+    scale = 1.0 / (width * SOFTMAX_TEMPER)
+    factor = LOSS_SCALE * scale
+    lanes_per_row = width // LANES
+
+    def columns(i, size):
+        return pl.ds(pl.multiple_of(i * size, size), size)
+
+    def score(dst, a, others):
+        dst[...] = jnp.zeros_like(dst)
+        chunk = 512
+
+        def body(i, carry):
+            at = columns(i, chunk)
+            dst[...] += lax.dot_general(
+                a[:, at], others[:, at], (((1,), (1,)), ((), ())), preferred_element_type=jnp.float32
+            )
+            return carry
+
+        lax.fori_loop(0, width // chunk, body, 0)
+        dst[...] = dst[...] * scale
+
+    def laid_out(k, n):
+        return floats[pl.ds(k, n, stride=lanes_per_row), :]
+
+    def as_row(column_values):
+        return jnp.transpose(jnp.broadcast_to(column_values, (rows, rows)))[0:1, :]
+
+    def finish(values, scales, dots, result):
+        scale_col = scales[...]
+        weight = scale_col * scale_col * scale_col * (jnp.sum(dots, 1, keepdims=True) / width)
+
+        def body(i, carry):
+            at = columns(i, 256)
+            result[:, at] = (
+                scale_col * unit[:, at] - weight * values[:, at].astype(jnp.float32)
+            ).astype(jnp.bfloat16)
+            return carry
+
+        lax.fori_loop(0, width // 256, body, 0)
+
+    def product(weight_rows, group):
+        def body(i, carry):
+            at = columns(i, 256)
+            unit[:, at] = jnp.dot(weight_rows, group[:, at], preferred_element_type=jnp.float32)
+            return carry
+
+        lax.fori_loop(0, width // 256, body, 0)
+
     q_spread(0, 0)
     for step in range(1, FAR + 1):
         for s in range(2):
-            q_hop(s, step).wait_recv()
-            if step < FAR:
-                q_hop(s, step + 1).start()
-        for s in range(2):
             p_step(s, FAR + 1 - step)
-        for s in range(2):
-            if step < FAR or s == 0:
-                q_spread(s, step)
+        if step > LAG:
+            q_step(step - LAG)
         if step == 2:
             pass_on(0)
-        if step == 4:
+        if step == 3:
             pass_on(1)
+        if step == 5:
+            x_end(0)
+            for copy in locals_:
+                copy.wait()
+            score(scores, qs, gp)
+            sums[...] = jnp.sum(jnp.exp(scores[...]), 1, keepdims=True)
+        if step == 6:
+            x_end(1)
+            score(scores_t, ps, gq)
 
     for s in range(2):
         p_hop(s, 1).wait_recv()
@@ -257,28 +323,112 @@
     pltpu.make_async_copy(here, here, py_recv.at[0, 0]).wait()
 
     def store(r, value):
-        hard[r] = value
+        floats[pl.ds(pl.multiple_of(r * lanes_per_row, lanes_per_row), lanes_per_row), :] = value.astype(
+            jnp.float32
+        )
 
     def load(r):
         return final[fin[r]]
 
     copy_rows(rows, store, load)
 
-    x_end(0)
-    x_end(1)
-    for copy in locals_:
+    dots = jnp.zeros((rows, LANES), jnp.float32)
+    for k in range(lanes_per_row):
+        dots += laid_out(k, rows) * qs[:, k * LANES : (k + 1) * LANES].astype(jnp.float32)
+    hard_score = jnp.sum(dots, 1, keepdims=True) * scale
+    totals = jnp.log(sums[...] + jnp.exp(hard_score))
+    hard_w = jnp.exp(hard_score - totals).astype(jnp.bfloat16).astype(jnp.float32)
+
+    ends[g, 0] = as_row(totals)
+    ends[g, 1] = flag[...]
+    weights[me, z] = as_row(hard_w)
+    t_copies = [remote(ends.at[g], ends.at[g], t_send.at[i], t_recv.at[i], sides[i]) for i in range(3)]
+    for copy in t_copies:
+        copy.start()
+    own_row = weights.at[me, z]
+    for device in lines:
+        remote(own_row, own_row, c_send.at[0], c_recv.at[0], device).start()
+
+    def settle(ref, sem):
+        pltpu.make_async_copy(ref, ref, sem).wait()
+
+    for d in range(FAR - LAG + 1, FAR):
+        q_step(d)
+
+    row_at = lax.broadcasted_iota(jnp.int32, scores.shape, 0)
+    col_at = lax.broadcasted_iota(jnp.int32, scores.shape, 1)
+    positive = jnp.where(col_at == row_at + g * rows, 1.0, 0.0)
+    product((jnp.exp(scores[...] - totals) - positive).astype(jnp.bfloat16), gp)
+    dots = jnp.zeros((rows, LANES), jnp.float32)
+    for k in range(lanes_per_row):
+        at = slice(k * LANES, (k + 1) * LANES)
+        value = (unit[:, at] + hard_w * laid_out(k, rows)) * factor
+        unit[:, at] = value
+        dots += queries[:, at].astype(jnp.float32) * value
+    finish(queries, qscale, dots, query_grad)
+
+    settle(weights.at[0, pl.ds(0, PLANES - 1)], c_recv.at[0])
+    own_line = weights.at[me]
+    for device in peers:
+        remote(own_line, own_line, c_send.at[1], c_recv.at[1], device).start()
+    q_step(FAR)
+
+    for copy in t_copies:
         copy.wait()
+    group_totals = jnp.concatenate([ends[i, 0] for i in range(n_grp)], axis=1)
+    flags[...] = jnp.maximum(jnp.maximum(ends[0, 1], ends[1, 1]), jnp.maximum(ends[2, 1], ends[3, 1]))
+    product((jnp.exp(scores_t[...] - group_totals) - positive).astype(jnp.bfloat16), gq)
+
+    settle(weights.at[pl.ds(0, PLANE - 1)], c_recv.at[1])
+    for who in range(PLANE):
+        for at in range(PLANES):
+            gathered[pl.ds(who * PLANES + at, 1), :] = weights[who, at]
+    lane = lax.broadcasted_iota(jnp.int32, (rows, LANES), 1)
+    placed = []
+    for k in range(SLOTS):
+        asker, offset = asked[:, 2 * k : 2 * k + 1], asked[:, 2 * k + 1 : 2 * k + 2]
+        slot_w = jnp.sum(jnp.where(lane == asker, gathered[...], 0.0), 1, keepdims=True)
+        placed.append(jnp.transpose(jnp.where(lane == offset, slot_w, 0.0)))
+    spread_w = jnp.concatenate(placed, axis=1).astype(jnp.bfloat16)
+
     for d in range(FAR + 1):
         for s in range(2):
             if (d == 0 or d == FAR) and s == 1:
                 continue
             line = 2 * d + s
             sent = qstage.at[line, pl.ds(SLOTS, OWN - SLOTS)]
-            pltpu.make_async_copy(sent, sent, qy_send.at[line]).wait()
-            pltpu.make_async_copy(sent, sent, qy_recv.at[line]).wait()
-            pltpu.make_async_copy(
-                qstage.at[line, pl.ds(0, SLOTS)], owed.at[pl.ds(0, SLOTS)], own_sem.at[2 + line]
-            ).wait()
+            settle(sent, qy_recv.at[line])
+            settle(qstage.at[line, pl.ds(0, SLOTS)], own_sem.at[2 + line])
+
+    for k in range(SLOTS):
+        for who in range(PLANE):
+            base = (k * PLANE + who) * PLANES * lanes_per_row
+
+            def widen(r, carry, k=k, who=who, base=base):
+                at = pl.multiple_of(base + r * lanes_per_row, lanes_per_row)
+                floats[pl.ds(at, lanes_per_row), :] = owed[k, who, r].astype(jnp.float32)
+                return carry
+
+            lax.fori_loop(0, PLANES, widen, 0)
+    dots = jnp.zeros((rows, LANES), jnp.float32)
+    for k in range(0, lanes_per_row, 2):
+        at = slice(k * LANES, (k + 2) * LANES)
+        pair = jnp.concatenate([laid_out(k, SLOTS * rows), laid_out(k + 1, SLOTS * rows)], axis=1)
+        value = unit[:, at] + jnp.dot(spread_w, pair.astype(jnp.bfloat16), preferred_element_type=jnp.float32)
+        value = value * factor
+        unit[:, at] = value
+        both = passages[:, at].astype(jnp.float32) * value
+        dots += both[:, :LANES] + both[:, LANES:]
+    finish(passages, pscale, dots, passage_grad)
+
+    settle(weights.at[0, pl.ds(0, PLANES - 1)], c_send.at[0])
+    settle(weights.at[pl.ds(0, PLANE - 1)], c_send.at[1])
+    for d in range(FAR + 1):
+        for s in range(2):
+            if (d == 0 or d == FAR) and s == 1:
+                continue
+            line = 2 * d + s
+            settle(qstage.at[line, pl.ds(SLOTS, OWN - SLOTS)], qy_send.at[line])
     for d in range(FAR + 1):
         for s in range(2):
             if d == 0 and s == 1:
@@ -290,49 +440,64 @@
                 p_hop(s, d).wait_send()
 
 
-def exchange(inv, srv, mrg, pick, fin, q3, p3, qs, ps):
-    rows, width = qs.shape
+def exchange(tables_, *arrays):
+    rows, width = arrays[2].shape
     line = (width // LANES, LANES)
-    slot_total = PLANES * PLANE * SLOTS
     smem = pl.BlockSpec(memory_space=pltpu.SMEM)
     vmem = pl.BlockSpec(memory_space=pltpu.VMEM)
-    hbm = pl.BlockSpec(memory_space=pl.ANY)
     dma = pltpu.SemaphoreType.DMA
 
     def buffer(*lead):
         return pltpu.VMEM(lead + line, jnp.bfloat16)
+
+    def wide(*shape):
+        return pltpu.VMEM(shape, jnp.float32)
 
     return pl.pallas_call(
         exchange_kernel,
         out_shape=(
-            jax.ShapeDtypeStruct((rows,) + line, jnp.bfloat16),
-            jax.ShapeDtypeStruct((slot_total,) + line, jnp.bfloat16),
-            jax.ShapeDtypeStruct((4 * rows, width), jnp.bfloat16),
-            jax.ShapeDtypeStruct((4 * rows, width), jnp.bfloat16),
+            jax.ShapeDtypeStruct((rows, width), jnp.bfloat16),
+            jax.ShapeDtypeStruct((rows, width), jnp.bfloat16),
+            jax.ShapeDtypeStruct((1, LANES), jnp.float32),
         ),
-        in_specs=[smem] * 5 + [vmem, vmem, hbm, hbm],
-        out_specs=(vmem, vmem, hbm, hbm),
+        in_specs=[smem] * 5 + [vmem] * 10,
+        out_specs=(vmem, vmem, vmem),
         scratch_shapes=[
+            pltpu.VMEM((4 * rows, width), jnp.bfloat16),
+            pltpu.VMEM((4 * rows, width), jnp.bfloat16),
             buffer(2, OUT_ROWS),
             buffer(2 * CAP1 + OWN),
             buffer(2, CAP1),
             buffer(2, FAR + 1, OWN),
             buffer(2 * (FAR + 1), OWN),
+            buffer(SLOTS, PLANE, PLANES),
+            wide(SLOTS * rows * line[0], LANES),
+            wide(rows, width),
+            wide(rows, 4 * rows),
+            wide(rows, 4 * rows),
+            wide(4, 2, 1, LANES),
+            wide(PLANE * PLANES, LANES),
+            wide(PLANE, PLANES, 1, LANES),
+            wide(rows, 1),
             dma((2 + 2 * (FAR + 1),)),
             dma((2, 4)), dma((2, 4)),
             dma((2, FAR + 1)), dma((2, FAR + 1)),
             dma((2, FAR + 1)), dma((2, FAR + 1)),
             dma((2, FAR + 1)), dma((2, FAR + 1)),
             dma((2 * (FAR + 1),)), dma((2 * (FAR + 1),)),
+            dma((3,)), dma((3,)),
+            dma((2,)), dma((2,)),
             *[buffer(OWN + CAPS[d + 1]) for _ in range(2) for d in range(1, FAR + 1)],
             *[buffer(CAPS[d]) for _ in range(2) for d in range(1, FAR + 1)],
         ],
         compiler_params=pltpu.CompilerParams(
-            collective_id=0, has_side_effects=True, vmem_limit_bytes=60 * 1024 * 1024
+            collective_id=0, has_side_effects=True, vmem_limit_bytes=62 * 1024 * 1024
         ),
-        cost_estimate=pl.CostEstimate(flops=0, bytes_accessed=40 * 1024 * 1024, transcendentals=0),
+        cost_estimate=pl.CostEstimate(
+            flops=2 * 2 * 2 * rows * 4 * rows * width, bytes_accessed=8 * 1024 * 1024, transcendentals=0
+        ),
         name="exchange",
-    )(inv, srv, mrg, pick, fin, q3, p3, qs, ps)
+    )(*tables_, *arrays)
 
 
 def column_kernel(x, full, here, plane_send, plane_recv, z_send, z_recv):
@@ -420,7 +585,7 @@
     cell = om * SLOTS + slot
     mine = oz == z
 
-    at = jnp.arange(CAP1)
+    at = jnp.arange(LANES)
     sides = jnp.arange(2)
     hit = (side[:, None, None, :] == sides[None, :, None, None]) & (
         pos[:, None, None, :] == at[None, None, :, None]
@@ -460,78 +625,115 @@
     first = jnp.where(count > 0, first, 0)
     codes = jnp.stack([first, last], 1)
     used = jnp.stack([count > 0, count > 1], 1)
-    return inv, codes % rows, mrg, pick, fin, codes // rows, used, own(owner) * SLOTS + own(slot)
-
-
-def padded(qshort, pshort, srv, home):
-    rows, width = qshort.shape
-    count = PLANES * PLANE
-
-    def swap(values):
-        moved = lax.all_to_all(
-            values.reshape(count, SLOTS, width), "batch", split_axis=0, concat_axis=0, tiled=True
-        )
-        return moved.reshape(count * SLOTS, width)
-
-    hard = jnp.take(swap(jnp.take(pshort, srv.reshape(-1), axis=0)), home, axis=0)
-    sender = jnp.sum(
-        jnp.where(jnp.arange(count * SLOTS)[:, None] == home[None, :], jnp.arange(rows)[None, :], 0), 1
-    )
-    return hard, swap(jnp.take(qshort, sender, axis=0))
+    asker = jnp.where(used, codes // rows, -1)
+    asked = jnp.stack([asker[:, 0], codes[:, 0] % rows, asker[:, 1], codes[:, 1] % rows], 1)
+    asked = asked.reshape(PLANES, PLANE, 4).transpose(1, 0, 2).reshape(-1, 4)
+    return inv, codes % rows, mrg, pick, fin, asked
+
+
+def padded(queries, passages, hard_ids):
+    pair_rows, embedding_dimension = queries.shape
+    batch_count = lax.axis_size("batch")
+    group_number_total = lax.axis_size("grp")
+    group_pos = lax.axis_index("grp")
+    capacity = 2 * ((pair_rows + batch_count - 1) // batch_count)
+    slot_total = batch_count * capacity
+    group_rows = group_number_total * pair_rows
+    inverse_permutation = 1.0 / (embedding_dimension * SOFTMAX_TEMPER)
+    factor = LOSS_SCALE * inverse_permutation
+    qscale = row_scales(queries)
+    pscale = row_scales(passages)
+    qshort = (queries.astype(jnp.float32) * qscale).astype(jnp.bfloat16)
+    pshort = (passages.astype(jnp.float32) * pscale).astype(jnp.bfloat16)
+    owners = hard_ids // pair_rows
+    offsets = hard_ids % pair_rows
+    local_rows = jnp.arange(pair_rows)
+    same_owner = owners[:, None] == owners[None, :]
+    earlier = local_rows[:, None] > local_rows[None, :]
+    rank_in = jnp.sum((same_owner & earlier).astype(jnp.int32), 1)
+    slot_index = owners * capacity + rank_in
+    slot_table = jnp.arange(slot_total)[:, None] == slot_index[None, :]
+    requests = jnp.sum(jnp.where(slot_table, offsets[None, :], 0), 1)
+    requests = requests.reshape(batch_count, capacity)
+    served_req = lax.all_to_all(requests, "batch", split_axis=0, concat_axis=0, tiled=True)
+    served_flat = served_req.reshape(-1)
+    served = jnp.take(pshort, served_flat, axis=0).reshape(
+        batch_count, capacity, embedding_dimension
+    )
+    arrived = lax.all_to_all(served, "batch", split_axis=0, concat_axis=0, tiled=True)
+    hard_p = jnp.take(arrived.reshape(slot_total, embedding_dimension), slot_index, axis=0)
+    group_p, group_q = (
+        lax.all_gather(pshort, "grp", axis=0, tiled=True),
+        lax.all_gather(qshort, "grp", axis=0, tiled=True),
+    )
+    own_cols = group_pos * pair_rows + local_rows
+    positive = (jnp.arange(group_rows)[None, :] == own_cols[:, None]).astype(jnp.float32)
+    inner_scores = (
+        jnp.dot(qshort, group_p.T, preferred_element_type=jnp.float32) * inverse_permutation
+    )
+    hard_score = (
+        jnp.einsum("rd,rd->r", qshort, hard_p, preferred_element_type=jnp.float32)
+        * inverse_permutation
+    )
+    totals = jnp.log(jnp.sum(jnp.exp(inner_scores), 1) + jnp.exp(hard_score))
+    inner_w = (jnp.exp(inner_scores - totals[:, None]) - positive).astype(jnp.bfloat16)
+    hard_w = jnp.exp(hard_score - totals).astype(jnp.bfloat16)
+    unit_q = (
+        jnp.dot(inner_w, group_p, preferred_element_type=jnp.float32)
+        + hard_w.astype(jnp.float32)[:, None] * hard_p
+    ) * factor
+    query_grad = norm_back(queries, qscale, unit_q).astype(jnp.bfloat16)
+    group_totals = lax.all_gather(totals, "grp", axis=0, tiled=True)
+    scores = jnp.dot(group_q, pshort.T, preferred_element_type=jnp.float32) * inverse_permutation
+    weight_factors = (jnp.exp(scores - group_totals[:, None]) - positive.T).astype(jnp.bfloat16)
+    unit_p = jnp.dot(weight_factors.T, group_q, preferred_element_type=jnp.float32) * factor
+    return_table = local_rows[:, None] == served_flat[None, :]
+    own_terms = hard_w.astype(jnp.float32)[:, None] * qshort * factor
+    term_slots = jnp.dot(
+        slot_table.astype(jnp.float32),
+        own_terms,
+        precision=lax.Precision.HIGHEST,
+        preferred_element_type=jnp.float32,
+    )
+    grad_terms = lax.all_to_all(
+        term_slots.reshape(batch_count, capacity, embedding_dimension).astype(jnp.bfloat16),
+        "batch",
+        split_axis=0,
+        concat_axis=0,
+        tiled=True,
+    ).astype(jnp.float32)
+    spread = jnp.dot(
+        return_table.astype(jnp.float32),
+        grad_terms.reshape(slot_total, embedding_dimension),
+        precision=lax.Precision.HIGHEST,
+        preferred_element_type=jnp.float32,
+    )
+    passage_grad = norm_back(passages, pscale, unit_p + spread).astype(jnp.bfloat16)
+    return (query_grad, passage_grad)
 
 
 def local(queries, passages, hard_ids):
     pair_rows, embedding_dimension = queries.shape
-    batch_count = lax.axis_size("batch")
-    group_rows = lax.axis_size("grp") * pair_rows
-    group_pos = lax.axis_index("grp")
-    scale = 1.0 / (embedding_dimension * SOFTMAX_TEMPER)
-    factor = LOSS_SCALE * scale
     line = (pair_rows, embedding_dimension // LANES, LANES)
+    b = lax.axis_index("batch")
 
     ids_all = column(hard_ids, 1, "hard_ids_column")
     qscale = row_scales(queries)
     pscale = row_scales(passages)
     qshort = (queries.astype(jnp.float32) * qscale).astype(jnp.bfloat16)
     pshort = (passages.astype(jnp.float32) * pscale).astype(jnp.bfloat16)
-    inv, srv, mrg, pick, fin, asker_row, used, home = tables(ids_all, lax.axis_index("batch"), pair_rows)
-    hard3, owed3, group_p, group_q = exchange(
-        inv, srv, mrg, pick, fin, qshort.reshape(line), pshort.reshape(line), qshort, pshort
-    )
-    hard_p, owed = lax.cond(
-        too_many(ids_all, pair_rows),
-        lambda: padded(qshort, pshort, srv, home),
-        lambda: (hard3.reshape(pair_rows, embedding_dimension), owed3.reshape(-1, embedding_dimension)),
-    )
-
-    local_rows = jnp.arange(pair_rows)
-    own_cols = group_pos * pair_rows + local_rows
-    positive = (jnp.arange(group_rows)[None, :] == own_cols[:, None]).astype(jnp.float32)
-    inner_scores = jnp.dot(qshort, group_p.T, preferred_element_type=jnp.float32) * scale
-    hard_score = jnp.sum(qshort.astype(jnp.float32) * hard_p.astype(jnp.float32), 1) * scale
-    totals = jnp.log(jnp.sum(jnp.exp(inner_scores), 1) + jnp.exp(hard_score))
-    hard_w = jnp.exp(hard_score - totals).astype(jnp.bfloat16)
-    group_totals = lax.all_gather(totals, "grp", axis=0, tiled=True)
-    weights_all = column(hard_w.astype(jnp.float32), 2, "weights_column")
-
-    inner_w = (jnp.exp(inner_scores - totals[:, None]) - positive).astype(jnp.bfloat16)
-    unit_q = (
-        jnp.dot(inner_w, group_p, preferred_element_type=jnp.float32)
-        + hard_w.astype(jnp.float32)[:, None] * hard_p
-    ) * factor
-    query_grad = norm_back(queries, qscale, unit_q).astype(jnp.bfloat16)
-
-    asked = asker_row[:, :, None] == local_rows[None, None, :]
-    slot_w = jnp.sum(jnp.where(asked & used[:, :, None], weights_all[:, None, :], 0.0), 2).reshape(-1)
-    spread_w = jnp.where(local_rows[:, None] == srv.reshape(-1)[None, :], slot_w[None, :], 0.0)
-    scores = jnp.dot(group_q, pshort.T, preferred_element_type=jnp.float32) * scale
-    inner_t = (jnp.exp(scores - group_totals[:, None]) - positive.T).astype(jnp.bfloat16)
-    unit_p = (
-        jnp.dot(inner_t.T, group_q, preferred_element_type=jnp.float32)
-        + jnp.dot(spread_w.astype(jnp.bfloat16), owed, preferred_element_type=jnp.float32)
-    ) * factor
-    passage_grad = norm_back(passages, pscale, unit_p).astype(jnp.bfloat16)
-    return (query_grad, passage_grad)
+    inv, srv, mrg, pick, fin, asked = tables(ids_all, b, pair_rows)
+    over = jnp.broadcast_to(too_many(ids_all, pair_rows).astype(jnp.float32), (1, LANES))
+    query_grad, passage_grad, flags = exchange(
+        (inv, srv, mrg, pick, fin),
+        qshort.reshape(line), pshort.reshape(line), qshort, pshort,
+        queries, passages, qscale, pscale, asked, over,
+    )
+    return lax.cond(
+        flags[0, 0] > 0,
+        lambda: padded(queries, passages, hard_ids),
+        lambda: (query_grad, passage_grad),
+    )
 
 
 def solution(mesh):

time: 271 us -> 249 us (0.919)
  matrix products: 17.8 us -> 0 us
  between operations: 1.67 us -> 15.5 us
  other arithmetic: 24.4 us -> 13.2 us
  blocking collectives: 8.39 us -> 0 us
  Pallas kernels: 204 us -> 210 us
    pallas_call x1, Pallas kernels: 154 us -> 183 us  [exchange(): pl.pallas_call(exchange_kernel, out_shape=(jax.ShapeDtypeStruct((rows, wi...]
    pallas_call x2 -> x1, Pallas kernels: 49.8 us -> 26.4 us  [column(): pl.pallas_call(column_kernel, out_shape=jax.ShapeDtypeStruct((PLANES * PL...]
    dot_general x4 -> x0, matrix products: 17.8 us -> none  [the longest x1 7.82 us: local(): jnp.dot(inner_t.T, group_q, preferred_element_type=jnp.float32)]
    all_gather x1 -> x0, blocking collectives: 8.39 us -> none  [local(): group_totals = lax.all_gather(totals, 'grp', axis=0, tiled=True)]
    another operation x5 -> x3, local copies, waits for them, and re-layouts: 5.9 us -> 0.31 us  [the longest x2 0.17 us: tables(): jnp.stack([asker[:, 0], codes[:, 0] % rows, asker[:, 1], codes[:, 1] % ro...]
    convert_element_type x4 -> x0, other arithmetic: 3.68 us -> none  [the longest x1 1.57 us: local(): passage_grad = norm_back(passages, pscale, unit_p).astype(jnp.bfloat16)]
    reduce_sum x2 -> x0, other arithmetic: 2.93 us -> none  [the longest x1 1.87 us: local(): jnp.sum(qshort.astype(jnp.float32) * hard_p.astype(jnp.float32), 1) * scale]
    unnamed x30 -> x18, local copies, waits for them, and re-layouts: 3.97 us -> 6 us
where the time goes in v2:
time: 249 us
  Pallas kernels  210 us (84%)
  between operations  15.5 us (6%)
  other arithmetic  13.2 us (5%)
  local copies, waits for them, and re-layouts  10.5 us (4%)
    pallas_call x1, Pallas kernels, exchange(): pl.pallas_call(exchange_kernel, out_shape=(jax.ShapeDtypeStruct((rows, wi...  183 us
    pallas_call x1, Pallas kernels, column(): pl.pallas_call(column_kernel, out_shape=jax.ShapeDtypeStruct((PLANES * PL...  26.4 us
    unnamed x18, local copies, waits for them, and re-layouts  6 us

profile of v2, /device:TPU:1, one launch (start us, length us, event | category | flops | bytes accessed | tf_op | source)
XLA Modules:
  0.0 249.1 jit_solution(16057721668713270914)
XLA Ops:
  7.2 26.4 %hard_ids_column.1 = s32[128,1,128]{2,1,0:T(1,128)} custom-call(s32[1,128]{1,0:T(1,128)} %bitcast.93), custom_call_target="tpu_custom_call" | custom-call | tf_op jit(solution)/shard_map/hard_ids_column/pallas_call | solution.py:539
  33.6 0.9 constant_dynamic-slice_fusion.3
  34.5 0.6 convert_reduce_fusion.2
  35.2 1.0 convert_reduce_fusion.3
  36.3 0.5 compare_select_fusion.38
  36.9 0.7 select_reduce_fusion.3.inv
  37.6 1.0 select_reduce_fusion.5
  38.6 0.1 copy.59
  38.8 0.1 copy.54
  38.9 0.7 fusion.39
  39.6 0.2 iota_compare_fusion.8
  39.7 0.8 select_reduce_fusion.1
  40.7 0.7 compare_select_fusion.20.mrg
  41.4 0.9 select_reduce_fusion.2.pick
  42.4 0.3 fusion.32
  42.7 0.3 fusion.34
  43.0 0.6 fusion.33
  43.6 1.4 copy.70
  45.0 1.2 copy.71
  46.2 0.7 copy.62.qscale
  47.0 0.7 copy.63.pscale
  47.9 0.2 slice_reduce_fusion.1
  48.2 0.1 stack.30
  48.3 0.8 copy.60
  49.1 1.5 compare_select_fusion.13
  50.7 2.3 convert_reduce_fusion.1
  53.0 0.7 select_reduce_fusion.6
  54.3 0.5 broadcast_in_dim.267.flag
  54.8 183.2 %exchange.1 = (bf16[128,4096]{1,0:T(8,128)(2,1)}, bf16[128,4096]{1,0:T(8,128)(2,1)}, f32[1,128]{1,0:T(1,128)}) custom-call(s32[2,128]{1,0:T(2,128)} %select_reduce_fusion.3.inv, s32[128,2]{1,0:T(8,128)} %get-tuple-element.55.srv, s32[16,2,128]{2,1,0:T(2,128)} %compare_select_fusion.20.mrg, s32[16,16]{1,0:T(8,128)} %select_reduce_fusion.2.pick, ...), custom_call_target="tpu_custom_call" | custom-call | flops 2147483648 | bytes 8388608 | tf_op jit(solution)/shard_map/exchange/pallas_call | solution.py:456
  238.6 0.3 conditional.1
  238.9 2.4 copy.78
  241.3 1.0 copy.79
  (49 shorter events, 0.8 us)
Async XLA Ops:
  7.2 35.2 %copy-start.3 = (bf16[128,4096]{1,0:T(8,128)(2,1)S(1)}, bf16[128,4096]{1,0:T(8,128)(2,1)}, u32[]{:S(2)}) copy-start(bf16[128,4096]{1,0:T(8,128)(2,1)} %queries.1) | copy-start | bytes 3145732
  7.2 35.5 %copy-start.2 = (bf16[128,4096]{1,0:T(8,128)(2,1)S(1)}, bf16[128,4096]{1,0:T(8,128)(2,1)}, u32[]{:S(2)}) copy-start(bf16[128,4096]{1,0:T(8,128)(2,1)} %passages.1) | copy-start | bytes 3145732
  43.6 2.7 %copy-start.8 = (bf16[128,4096]{1,0:T(8,128)(2,1)}, bf16[128,4096]{1,0:T(8,128)(2,1)S(1)}, u32[]{:S(2)}) copy-start(bf16[128,4096]{1,0:T(8,128)(2,1)S(1)} %get-tuple-element.76.qs) | copy-start | bytes 3145732
  43.6 2.7 %copy-start.9 = (bf16[128,4096]{1,0:T(8,128)(2,1)}, bf16[128,4096]{1,0:T(8,128)(2,1)S(1)}, u32[]{:S(2)}) copy-start(bf16[128,4096]{1,0:T(8,128)(2,1)S(1)} %get-tuple-element.77.ps) | copy-start | bytes 3145732
  43.6 5.5 %copy-start.12 = (s32[128,1,128]{2,1,0:T(1,128)S(1)}, s32[128,1,128]{2,1,0:T(1,128)}, u32[]{:S(2)}) copy-start(s32[128,1,128]{2,1,0:T(1,128)} %hard_ids_column.1) | copy-start | bytes 196612
  54.8 183.8 %copy-start.13 = (s32[128]{0:T(128)S(1)}, s32[128]{0:T(128)}, u32[]{:S(2)}) copy-start(s32[128]{0:T(128)} %param.7) | copy-start | bytes 1540
  238.9 2.4 copy-start.11

commit v3 on v2

v3 whole, which is shorter than its diff:
```python
import functools

import jax
import jax.numpy as jnp
from jax import lax
from jax.experimental import pallas as pl
from jax.experimental.pallas import tpu as pltpu
from jax.sharding import PartitionSpec as P

SOFTMAX_TEMPER = 0.02
LOSS_SCALE = 64.0
EPSILON = 1e-06

PLANES = 16
PLANE = 8
FAR = PLANES // 2
SLOTS = 2
OWN = PLANE * SLOTS
CAPS = [0, 84, 76, 68, 60, 50, 38, 24, 8, 0]
LANES = 128
Q_AT = {1: (2,), 3: (3,), 5: (4,), 6: (5,), 7: (6,)}


def row_scales(values):
    floats = values.astype(jnp.float32)
    return lax.rsqrt(jnp.mean(floats * floats, -1, keepdims=True) + EPSILON)


def norm_back(values, scales, upstream):
    floats = values.astype(jnp.float32)
    return scales * upstream - scales * scales * scales * floats * jnp.mean(
        floats * upstream, -1, keepdims=True
    )


def offsets_of(sizes):
    out, total = [], 0
    for size in sizes:
        out.append(total)
        total += size
    return out, total


OUT_AT, OUT_ROWS = offsets_of([0] + [CAPS[d] for d in range(1, FAR + 1)])
CAP1 = CAPS[1]
SPLIT = 40


def parts_of(d):
    return [c for c in range(2) if CAPS[d] > c * SPLIT]


def part_of(d, c):
    return c * SPLIT, (CAPS[d] - SPLIT if c else min(CAPS[d], SPLIT))


def exchange_kernel(
    ids, queries, passages,
    query_grad, passage_grad, flags,
    q3, p3, qs, ps, qscale, pscale, column_ids, ids2, line_table, own_table, slot_table, asked,
    line_at, own_at, slot_at,
    gp, gq, out, final, qfirst, pstage, qstage, owed, floats, unit, scores, scores_t,
    ends, gathered, weights, sums,
    own_sem, x_send, x_recv, qz_send, qz_recv, pz_send, pz_recv,
    py_send, py_recv, qy_send, qy_recv, t_send, t_recv, c_send, c_recv, i_send, i_recv, table_sem, *arriving
):
    own = [[None, *arriving[(4 + s) * FAR : (5 + s) * FAR]] for s in range(2)]
    comb = [[None, *arriving[s * FAR : (s + 1) * FAR]] for s in range(2)]
    qin = [[None, *arriving[(2 + s) * FAR : (3 + s) * FAR]] for s in range(2)]
    rows, width = queries.shape
    lanes_per_row = width // LANES
    half = rows // 2
    b = lax.axis_index("batch")
    g = lax.axis_index("grp")
    n_grp = 4
    z, me = b // PLANE, b % PLANE

    def plane(step):
        return lax.rem(z + step + PLANES, PLANES)

    def peer(j):
        return lax.rem(me + j, PLANE)

    lines = [{"batch": plane(j) * PLANE + me} for j in range(1, PLANES)]
    ahead = [lines[0], lines[-1]]
    right, left = lax.rem(g + 1, n_grp), lax.rem(g + n_grp - 1, n_grp)
    sides = [{"grp": right}, {"grp": left}]
    peers = [{"batch": z * PLANE + peer(j)} for j in range(1, PLANE)]

    barrier = pltpu.get_barrier_semaphore()
    across = lax.rem(g + 2, n_grp)
    sides.append({"grp": across})
    greeted = lines + sides + peers
    for device in greeted:
        pl.semaphore_signal(barrier, inc=1, device_id=device, device_id_type=pl.DeviceIdType.MESH)

    def columns(i, size):
        return pl.ds(pl.multiple_of(i * size, size), size)

    def unit_rows(values, scales, short, spread):
        def square(i, total):
            part = values[:, columns(i, 256)].astype(jnp.float32)
            part = part * part
            return total + part[:, :LANES] + part[:, LANES:]

        total = lax.fori_loop(0, width // 256, square, jnp.zeros((rows, LANES), jnp.float32))
        scale_col = lax.rsqrt(jnp.sum(total, 1, keepdims=True) / width + EPSILON)
        scales[...] = scale_col
        for k in range(lanes_per_row):
            at = slice(k * LANES, (k + 1) * LANES)
            part = (values[:, at].astype(jnp.float32) * scale_col).astype(jnp.bfloat16)
            short[:, at] = part
            floats[pl.ds(k, rows, stride=lanes_per_row), :] = part.astype(jnp.float32)

        def narrow(r, carry):
            at = pl.ds(pl.multiple_of(r * lanes_per_row, lanes_per_row), lanes_per_row)
            spread[r] = floats[at, :].astype(jnp.bfloat16)
            return carry

        lax.fori_loop(0, rows, narrow, 0)

    sub = lax.broadcasted_iota(jnp.int32, (rows, LANES), 0)
    lane = lax.broadcasted_iota(jnp.int32, (rows, LANES), 1)

    def course_of(values, plane_of, me_of):
        oz, om = values >> 10, (values >> 7) & (PLANE - 1)
        ahead_of = (plane_of - oz) & (PLANES - 1)
        tie = (om + me_of) & 1
        side = jnp.where(ahead_of == 0, 2, jnp.where(ahead_of < FAR, 0, jnp.where(ahead_of == FAR, tie, 1)))
        return oz, om, side, jnp.where(ahead_of <= FAR, ahead_of, PLANES - ahead_of)

    def as_column(row):
        wide_row = jnp.broadcast_to(row.astype(jnp.float32), (rows, rows))
        return jnp.transpose(wide_row).astype(jnp.int32)

    def count_lanes(mask):
        return jnp.sum(jnp.where(mask, 1.0, 0.0), 1, keepdims=True).astype(jnp.int32)

    def pick_row(mask, values):
        return jnp.sum(jnp.where(mask, values.astype(jnp.float32), 0.0), 0, keepdims=True).astype(jnp.int32)

    def requests(row, plane_of):
        row = jnp.broadcast_to(row, (rows, LANES))
        col = as_column(row[0:1])
        _, _, side_r, dist_r = course_of(row, plane_of, me)
        oz, om, side, dist = course_of(col, plane_of, me)
        code_r = dist_r * LANES + (LANES - 1) - lane
        code = dist * LANES + (LANES - 1) - sub
        pos = count_lanes((side_r == side) & (code_r > code))
        slot = count_lanes(((row >> 7) == (col >> 7)) & (lane < sub))
        return oz, side, jnp.broadcast_to(pos, (rows, LANES)), om * SLOTS + jnp.minimum(slot, SLOTS - 1)

    unit_rows(queries, qscale, qs, q3)
    _, my_side, my_pos, my_cell = requests(ids[...], z)
    for s in range(2):
        own_table[s : s + 1, :] = jnp.minimum(pick_row((my_side == s) & (my_pos == lane), sub), rows - 1)
    home = jnp.where(my_side == 2, 2 * CAP1 + my_cell, my_side * CAP1 + jnp.minimum(my_pos, CAP1 - 1))
    own_table[2:3, :] = pick_row(sub == lane, home)
    own_copy = pltpu.make_async_copy(own_table, own_at, table_sem.at[0])
    own_copy.start()
    column_ids[b] = ids[...]
    pl.semaphore_wait(barrier, len(greeted))

    def remote(src, dst, send, recv, device):
        return pltpu.make_async_remote_copy(
            src_ref=src, dst_ref=dst, send_sem=send, recv_sem=recv,
            device_id=device, device_id_type=pl.DeviceIdType.MESH,
        )

    def settle(ref, sem):
        pltpu.make_async_copy(ref, ref, sem).wait()

    own_ids = column_ids.at[b]
    for device in peers:
        remote(own_ids, own_ids, i_send.at[0], i_recv.at[0], device).start()

    def block(ref, who, start=0, size=rows):
        return ref.at[pl.ds(pl.multiple_of(who * rows + start, half), size), :]

    whole = ((ps, gp), (qs, gq))
    locals_ = []

    def pass_on(a):
        dst = whole[a][1]
        for s, origin in ((0, left), (1, right)):
            remote(ps, block(dst, origin), x_send.at[a, s], x_recv.at[a, s], sides[s]).wait_recv()
            part = block(dst, origin, s * half, half)
            remote(part, part, x_send.at[a, 2 + s], x_recv.at[a, 2 + s], sides[s]).start()

    def x_end(a):
        dst = whole[a][1]
        for s in range(2):
            part = block(dst, across, s * half, half)
            remote(part, part, x_send.at[a, 2 + s], x_recv.at[a, 2 + s], sides[s]).wait()
            remote(ps, block(dst, g), x_send.at[a, s], x_recv.at[a, s], sides[s]).wait_send()

    def inside(at, count):
        return jnp.maximum(jnp.minimum(at, count - 1), 0)

    def copy_rows(n, store, load):
        def body(r, carry):
            store(r, load(r))
            return carry

        lax.fori_loop(0, n, body, 0, unroll=False)

    def q_hop(s, d, c):
        low, size = part_of(d, c)
        src = qfirst.at[s] if d == 1 else qin[s][d - 1]
        at = pl.ds(low, size)
        return remote(src.at[at], qin[s][d].at[at], qz_send.at[s, d, c], qz_recv.at[s, d, c], ahead[1 - s])

    own_copy.wait()
    for s in range(2):
        def store(r, value, s=s):
            qfirst[s, r] = value

        def load(r, s=s):
            return q3[inside(own_at[s, r], rows)]

        copy_rows(CAP1, store, load)
        for c in parts_of(1):
            q_hop(s, 1, c).start()

    settle(column_ids.at[pl.ds(0, PLANE - 1)], i_recv.at[0])
    plane_ids = column_ids.at[pl.ds(z * PLANE, PLANE)]
    for device in lines:
        remote(plane_ids, plane_ids, i_send.at[1], i_recv.at[1], device).start()
    unit_rows(passages, pscale, ps, p3)

    for a, (src, dst) in enumerate(whole):
        copy = pltpu.make_async_copy(src, block(dst, g), own_sem.at[a])
        copy.start()
        locals_.append(copy)
        for s in range(2):
            remote(src, block(dst, g), x_send.at[a, s], x_recv.at[a, s], sides[s]).start()

    settle(column_ids.at[pl.ds(0, PLANE * (PLANES - 1))], i_recv.at[1])

    def flat(r, carry):
        ids2[pl.ds(r, 1), :] = column_ids[r]
        return carry

    lax.fori_loop(0, PLANES * PLANE, flat, 0)

    wanted = (ids2[...] >> 7) == b
    code = (lane * LANES + (ids2[...] & (LANES - 1))).astype(jnp.float32)
    asks = count_lanes(wanted)
    first = jnp.min(jnp.where(wanted, code, float(LANES * LANES)), 1, keepdims=True).astype(jnp.int32)
    last = jnp.max(jnp.where(wanted, code, 0.0), 1, keepdims=True).astype(jnp.int32)
    first = jnp.where(asks > 0, first, 0)
    askers = [jnp.where(asks > 0, first >> 7, -1), jnp.where(asks > 1, last >> 7, -1)]
    offsets = [first & (LANES - 1), last & (LANES - 1)]
    slot_table[...] = jnp.where(lane == 0, offsets[0], offsets[1])
    slot_copy = pltpu.make_async_copy(slot_table, slot_at, table_sem.at[1])
    slot_copy.start()
    asked[...] = jnp.where(
        lane == 0, askers[0], jnp.where(lane == 1, offsets[0], jnp.where(lane == 2, askers[1], offsets[1]))
    )

    def line_rows(source, carry):
        oz, side, pos, cell = requests(ids2[pl.ds(source * PLANE + me, 1), :], source)
        here = oz == z
        for s in range(2):
            hit = here & (side == s) & (pos == lane)
            placed = jnp.minimum(pick_row(hit, cell + 1) - 1, OWN - 1)
            far = lax.rem((source - z if s == 0 else z - source) + PLANES, PLANES)
            room = 0
            for d in range(1, FAR):
                room = jnp.where(far == d, CAPS[d + 1], room)
            filler = SLOTS * peer(s)
            other = jnp.where(lane[0:1] < room, OWN, filler)
            line_table[pl.ds(s * PLANES + source, 1), :] = jnp.where(placed >= 0, placed, other)
        place = jnp.where(side == 2, sub, pos)
        far = lax.rem(source - z + PLANES, PLANES)
        limit = rows - 1
        for d in range(1, FAR + 1):
            limit = jnp.where((far == d) | (far == PLANES - d), CAPS[d] - 1, limit)
        line_table[pl.ds(2 * PLANES + source, 1), :] = jnp.minimum(pick_row(here & (cell == lane), place), limit)
        return carry

    lax.fori_loop(0, PLANES, line_rows, 0)
    line_copy = pltpu.make_async_copy(line_table, line_at, table_sem.at[2])
    line_copy.start()
    slot_copy.wait()
    line_copy.wait()

    def p_owed(s, d):
        return plane(d) if s == 0 else plane(-d)

    def partners(s, d):
        return range(s, PLANE, 2) if d == FAR else range(PLANE)

    def p_spread(s, d):
        target = p_owed(s, d)
        place = pl.ds(me * SLOTS, SLOTS)
        others = 0
        for j in partners(s, d):
            for k in range(SLOTS):
                row = p3[inside(slot_at[target * PLANE + peer(j), k], rows)]
                if j == 0:
                    own[s][d][me * SLOTS + k] = row
                else:
                    pstage[s, d, others * SLOTS + k] = row
            if j:
                others += 1
        others = 0
        for j in partners(s, d):
            if j:
                remote(
                    pstage.at[s, d, pl.ds(others * SLOTS, SLOTS)], own[s][d].at[place],
                    py_send.at[s, d], py_recv.at[s, d], peers[j - 1],
                ).start()
                others += 1

    def p_spread_near():
        near = 2 * CAP1
        for k in range(SLOTS):
            final[near + me * SLOTS + k] = p3[inside(slot_at[z * PLANE + me, k], rows)]
        for j in range(1, PLANE):
            for k in range(SLOTS):
                pstage[0, 0, (j - 1) * SLOTS + k] = p3[inside(slot_at[z * PLANE + peer(j), k], rows)]
        for j in range(1, PLANE):
            remote(
                pstage.at[0, 0, pl.ds((j - 1) * SLOTS, SLOTS)],
                final.at[pl.ds(near + me * SLOTS, SLOTS)],
                py_send.at[0, 0], py_recv.at[0, 0], peers[j - 1],
            ).start()

    def spread_bytes(s, d):
        n = SLOTS * len([j for j in partners(s, d) if j])
        return pstage.at[s, d, pl.ds(0, n)]

    for d in range(FAR, 0, -1):
        for s in range(2):
            p_spread(s, d)
    p_spread_near()

    def p_hop(s, d, c):
        low, size = part_of(d, c)
        src = out.at[s, pl.ds(OUT_AT[d] + low, size)]
        dst = final.at[pl.ds(s * CAP1 + low, size)] if d == 1 else comb[s][d - 1].at[pl.ds(low, size)]
        return remote(src, dst, pz_send.at[s, d, c], pz_recv.at[s, d, c], ahead[s])

    def p_step(s, d, c):
        if c == 0:
            settle(spread_bytes(s, d), py_recv.at[s, d])
        low, size = part_of(d, c)
        target = p_owed(s, d)
        passing = 0
        if c in parts_of(d + 1):
            p_hop(s, d + 1, c).wait_recv()
            passing = part_of(d + 1, c)[1]

        def cell(r):
            return line_at[s * PLANES + target, r]

        def store(r, value):
            out[s, OUT_AT[d] + low + r] = value

        def load(r):
            at = cell(low + r)
            here = own[s][d][inside(at, OWN)]
            return lax.select(at < OWN, here, comb[s][d][low + r])

        copy_rows(passing, store, load)

        def store_new(r, value):
            out[s, OUT_AT[d] + low + passing + r] = value

        def load_new(r):
            return own[s][d][inside(cell(low + passing + r), OWN)]

        copy_rows(size - passing, store_new, load_new)
        p_hop(s, d, c).start()

    def q_spread(s, d):
        source = plane(d) if s == 0 else plane(-d)

        def take(j, k):
            at = line_at[2 * PLANES + source, peer(j) * SLOTS + k]
            if d == 0:
                return q3[inside(at, rows)]
            return qin[j % 2 if d == FAR else s][d][inside(at, CAPS[d])]

        place = owed.at[:, source, me]
        line = 2 * d + s
        for j in range(PLANE):
            for k in range(SLOTS):
                qstage[line, j * SLOTS + k] = take(j, k)
        pltpu.make_async_copy(
            qstage.at[line, pl.ds(0, SLOTS)], place, own_sem.at[2 + line]
        ).start()
        for j in range(1, PLANE):
            remote(
                qstage.at[line, pl.ds(j * SLOTS, SLOTS)], place,
                qy_send.at[line], qy_recv.at[line], peers[j - 1],
            ).start()

    def q_step(d):
        for c in parts_of(d):
            for s in range(2):
                q_hop(s, d, c).wait_recv()
                if c in parts_of(d + 1):
                    q_hop(s, d + 1, c).start()
        for s in range(2):
            if d < FAR or s == 0:
                q_spread(s, d)

    scale = 1.0 / (width * SOFTMAX_TEMPER)
    factor = LOSS_SCALE * scale

    def score(dst, a, others):
        dst[...] = jnp.zeros_like(dst)
        chunk = 512

        def body(i, carry):
            at = columns(i, chunk)
            dst[...] += lax.dot_general(
                a[:, at], others[:, at], (((1,), (1,)), ((), ())), preferred_element_type=jnp.float32
            )
            return carry

        lax.fori_loop(0, width // chunk, body, 0)
        dst[...] = dst[...] * scale

    def laid_out(k, n):
        return floats[pl.ds(k, n, stride=lanes_per_row), :]

    def as_row(column_values):
        return jnp.transpose(jnp.broadcast_to(column_values, (rows, rows)))[0:1, :]

    def finish(values, scales, dots, result):
        scale_col = scales[...]
        weight = scale_col * scale_col * scale_col * (jnp.sum(dots, 1, keepdims=True) / width)

        def body(i, carry):
            at = columns(i, 256)
            result[:, at] = (
                scale_col * unit[:, at] - weight * values[:, at].astype(jnp.float32)
            ).astype(jnp.bfloat16)
            return carry

        lax.fori_loop(0, width // 256, body, 0)

    def product(weight_rows, group):
        def body(i, carry):
            at = columns(i, 256)
            unit[:, at] = jnp.dot(weight_rows, group[:, at], preferred_element_type=jnp.float32)
            return carry

        lax.fori_loop(0, width // 256, body, 0)

    q_spread(0, 0)
    q_step(1)
    for step in range(1, FAR + 1):
        for c in parts_of(FAR + 1 - step):
            for s in range(2):
                p_step(s, FAR + 1 - step, c)
        for d in Q_AT.get(step, ()):
            q_step(d)
        if step == 2:
            pass_on(0)
        if step == 3:
            pass_on(1)
        if step == 5:
            x_end(0)
            for copy in locals_:
                copy.wait()
            score(scores, qs, gp)
            sums[...] = jnp.sum(jnp.exp(scores[...]), 1, keepdims=True)
        if step == 4:
            who = (sub >> 3, sub & (PLANE - 1))
            _, _, side, dist = course_of(ids2[...], *who)
            over = jnp.zeros((rows, 1), jnp.float32)
            for s in range(2):
                for d in range(1, FAR):
                    over = jnp.maximum(over, jnp.where(count_lanes((side == s) & (dist >= d)) > CAPS[d], 1.0, 0.0))
            flag = jnp.max(jnp.broadcast_to(over, (rows, LANES)), 0, keepdims=True)
        if step == 6:
            x_end(1)
            score(scores_t, ps, gq)

    for s in range(2):
        for c in parts_of(1):
            p_hop(s, 1, c).wait_recv()
    here = spread_bytes(0, 0)
    pltpu.make_async_copy(here, here, py_recv.at[0, 0]).wait()

    def store(r, value):
        floats[pl.ds(pl.multiple_of(r * lanes_per_row, lanes_per_row), lanes_per_row), :] = value.astype(
            jnp.float32
        )

    def load(r):
        return final[inside(own_at[2, r], 2 * CAP1 + OWN)]

    copy_rows(rows, store, load)

    dots = jnp.zeros((rows, LANES), jnp.float32)
    for k in range(lanes_per_row):
        dots += laid_out(k, rows) * qs[:, k * LANES : (k + 1) * LANES].astype(jnp.float32)
    hard_score = jnp.sum(dots, 1, keepdims=True) * scale
    totals = jnp.log(sums[...] + jnp.exp(hard_score))
    hard_w = jnp.exp(hard_score - totals).astype(jnp.bfloat16).astype(jnp.float32)

    ends[g, 0] = as_row(totals)
    ends[g, 1] = flag
    weights[me, z] = as_row(hard_w)
    t_copies = [remote(ends.at[g], ends.at[g], t_send.at[i], t_recv.at[i], sides[i]) for i in range(3)]
    for copy in t_copies:
        copy.start()
    own_row = weights.at[me, z]
    for device in lines:
        remote(own_row, own_row, c_send.at[0], c_recv.at[0], device).start()

    q_step(FAR - 1)

    row_at = lax.broadcasted_iota(jnp.int32, scores.shape, 0)
    col_at = lax.broadcasted_iota(jnp.int32, scores.shape, 1)
    positive = jnp.where(col_at == row_at + g * rows, 1.0, 0.0)
    product((jnp.exp(scores[...] - totals) - positive).astype(jnp.bfloat16), gp)
    dots = jnp.zeros((rows, LANES), jnp.float32)
    for k in range(lanes_per_row):
        at = slice(k * LANES, (k + 1) * LANES)
        value = (unit[:, at] + hard_w * laid_out(k, rows)) * factor
        unit[:, at] = value
        dots += queries[:, at].astype(jnp.float32) * value
    finish(queries, qscale, dots, query_grad)

    settle(weights.at[0, pl.ds(0, PLANES - 1)], c_recv.at[0])
    own_line = weights.at[me]
    for device in peers:
        remote(own_line, own_line, c_send.at[1], c_recv.at[1], device).start()
    q_step(FAR)

    for copy in t_copies:
        copy.wait()
    group_totals = jnp.concatenate([ends[i, 0] for i in range(n_grp)], axis=1)
    flags[...] = jnp.maximum(jnp.maximum(ends[0, 1], ends[1, 1]), jnp.maximum(ends[2, 1], ends[3, 1]))
    product((jnp.exp(scores_t[...] - group_totals) - positive).astype(jnp.bfloat16), gq)

    settle(weights.at[pl.ds(0, PLANE - 1)], c_recv.at[1])
    for who in range(PLANE):
        for at in range(PLANES):
            gathered[pl.ds(at * PLANE + who, 1), :] = weights[who, at]
    placed = []
    for k in range(SLOTS):
        asker, offset = asked[:, 2 * k : 2 * k + 1], asked[:, 2 * k + 1 : 2 * k + 2]
        slot_w = jnp.sum(jnp.where(lane == asker, gathered[...], 0.0), 1, keepdims=True)
        placed.append(jnp.transpose(jnp.where(lane == offset, slot_w, 0.0)))
    spread_w = jnp.concatenate(placed, axis=1).astype(jnp.bfloat16)

    for d in range(FAR + 1):
        for s in range(2):
            if (d == 0 or d == FAR) and s == 1:
                continue
            line = 2 * d + s
            sent = qstage.at[line, pl.ds(SLOTS, OWN - SLOTS)]
            settle(sent, qy_recv.at[line])
            settle(qstage.at[line, pl.ds(0, SLOTS)], own_sem.at[2 + line])

    for k in range(SLOTS):
        for who in range(PLANE):

            def widen(r, carry, k=k, who=who):
                at = pl.multiple_of(((k * PLANES + r) * PLANE + who) * lanes_per_row, lanes_per_row)
                floats[pl.ds(at, lanes_per_row), :] = owed[k, r, who].astype(jnp.float32)
                return carry

            lax.fori_loop(0, PLANES, widen, 0)
    dots = jnp.zeros((rows, LANES), jnp.float32)
    for k in range(0, lanes_per_row, 2):
        at = slice(k * LANES, (k + 2) * LANES)
        pair = jnp.concatenate([laid_out(k, SLOTS * rows), laid_out(k + 1, SLOTS * rows)], axis=1)
        value = unit[:, at] + jnp.dot(spread_w, pair.astype(jnp.bfloat16), preferred_element_type=jnp.float32)
        value = value * factor
        unit[:, at] = value
        both = passages[:, at].astype(jnp.float32) * value
        dots += both[:, :LANES] + both[:, LANES:]
    finish(passages, pscale, dots, passage_grad)

    settle(column_ids.at[pl.ds(0, PLANE - 1)], i_send.at[0])
    settle(column_ids.at[pl.ds(0, PLANE * (PLANES - 1))], i_send.at[1])
    settle(weights.at[0, pl.ds(0, PLANES - 1)], c_send.at[0])
    settle(weights.at[pl.ds(0, PLANE - 1)], c_send.at[1])
    for d in range(FAR + 1):
        for s in range(2):
            if (d == 0 or d == FAR) and s == 1:
                continue
            line = 2 * d + s
            settle(qstage.at[line, pl.ds(SLOTS, OWN - SLOTS)], qy_send.at[line])
    for d in range(FAR + 1):
        for s in range(2):
            if d == 0 and s == 1:
                continue
            here = spread_bytes(s, d)
            pltpu.make_async_copy(here, here, py_send.at[s, d]).wait()
            if d > 0:
                for c in parts_of(d):
                    q_hop(s, d, c).wait_send()
                    p_hop(s, d, c).wait_send()


def exchange(ids, queries, passages):
    rows, width = queries.shape
    line = (width // LANES, LANES)
    vmem = pl.BlockSpec(memory_space=pltpu.VMEM)
    dma = pltpu.SemaphoreType.DMA

    def buffer(*lead):
        return pltpu.VMEM(lead + line, jnp.bfloat16)

    def wide(*shape):
        return pltpu.VMEM(shape, jnp.float32)

    def table(*shape):
        return pltpu.VMEM(shape, jnp.int32)

    return pl.pallas_call(
        exchange_kernel,
        out_shape=(
            jax.ShapeDtypeStruct((rows, width), jnp.bfloat16),
            jax.ShapeDtypeStruct((rows, width), jnp.bfloat16),
            jax.ShapeDtypeStruct((1, LANES), jnp.float32),
        ),
        in_specs=[vmem] * 3,
        out_specs=(vmem, vmem, vmem),
        scratch_shapes=[
            buffer(rows),
            buffer(rows),
            pltpu.VMEM((rows, width), jnp.bfloat16),
            pltpu.VMEM((rows, width), jnp.bfloat16),
            wide(rows, 1),
            wide(rows, 1),
            table(PLANES * PLANE, 1, LANES),
            table(PLANES * PLANE, LANES),
            table(3 * PLANES, LANES),
            table(8, LANES),
            table(PLANES * PLANE, LANES),
            table(PLANES * PLANE, LANES),
            pltpu.SMEM((3 * PLANES, LANES), jnp.int32),
            pltpu.SMEM((8, LANES), jnp.int32),
            pltpu.SMEM((PLANES * PLANE, LANES), jnp.int32),
            pltpu.VMEM((4 * rows, width), jnp.bfloat16),
            pltpu.VMEM((4 * rows, width), jnp.bfloat16),
            buffer(2, OUT_ROWS),
            buffer(2 * CAP1 + OWN),
            buffer(2, CAP1),
            buffer(2, FAR + 1, OWN),
            buffer(2 * (FAR + 1), OWN),
            buffer(SLOTS, PLANES, PLANE),
            wide(SLOTS * rows * line[0], LANES),
            wide(rows, width),
            wide(rows, 4 * rows),
            wide(rows, 4 * rows),
            wide(4, 2, 1, LANES),
            wide(PLANE * PLANES, LANES),
            wide(PLANE, PLANES, 1, LANES),
            wide(rows, 1),
            dma((2 + 2 * (FAR + 1),)),
            dma((2, 4)), dma((2, 4)),
            dma((2, FAR + 1, 2)), dma((2, FAR + 1, 2)),
            dma((2, FAR + 1, 2)), dma((2, FAR + 1, 2)),
            dma((2, FAR + 1)), dma((2, FAR + 1)),
            dma((2 * (FAR + 1),)), dma((2 * (FAR + 1),)),
            dma((3,)), dma((3,)),
            dma((2,)), dma((2,)),
            dma((2,)), dma((2,)), dma((3,)),
            *[buffer(max(CAPS[d + 1], OWN)) for _ in range(2) for d in range(1, FAR + 1)],
            *[buffer(CAPS[d]) for _ in range(2) for d in range(1, FAR + 1)],
            *[buffer(OWN) for _ in range(2 * FAR)],
        ],
        compiler_params=pltpu.CompilerParams(
            collective_id=0, has_side_effects=True, vmem_limit_bytes=62 * 1024 * 1024
        ),
        cost_estimate=pl.CostEstimate(
            flops=2 * 2 * 2 * rows * 4 * rows * width, bytes_accessed=8 * 1024 * 1024, transcendentals=0
        ),
        name="exchange",
    )(ids, queries, passages)


def padded(queries, passages, hard_ids):
    pair_rows, embedding_dimension = queries.shape
    batch_count = lax.axis_size("batch")
    group_number_total = lax.axis_size("grp")
    group_pos = lax.axis_index("grp")
    capacity = 2 * ((pair_rows + batch_count - 1) // batch_count)
    slot_total = batch_count * capacity
    group_rows = group_number_total * pair_rows
    inverse_permutation = 1.0 / (embedding_dimension * SOFTMAX_TEMPER)
    factor = LOSS_SCALE * inverse_permutation
    qscale = row_scales(queries)
    pscale = row_scales(passages)
    qshort = (queries.astype(jnp.float32) * qscale).astype(jnp.bfloat16)
    pshort = (passages.astype(jnp.float32) * pscale).astype(jnp.bfloat16)
    owners = hard_ids // pair_rows
    offsets = hard_ids % pair_rows
    local_rows = jnp.arange(pair_rows)
    same_owner = owners[:, None] == owners[None, :]
    earlier = local_rows[:, None] > local_rows[None, :]
    rank_in = jnp.sum((same_owner & earlier).astype(jnp.int32), 1)
    slot_index = owners * capacity + rank_in
    slot_table = jnp.arange(slot_total)[:, None] == slot_index[None, :]
    requests = jnp.sum(jnp.where(slot_table, offsets[None, :], 0), 1)
    requests = requests.reshape(batch_count, capacity)
    served_req = lax.all_to_all(requests, "batch", split_axis=0, concat_axis=0, tiled=True)
    served_flat = served_req.reshape(-1)
    served = jnp.take(pshort, served_flat, axis=0).reshape(
        batch_count, capacity, embedding_dimension
    )
    arrived = lax.all_to_all(served, "batch", split_axis=0, concat_axis=0, tiled=True)
    hard_p = jnp.take(arrived.reshape(slot_total, embedding_dimension), slot_index, axis=0)
    group_p, group_q = (
        lax.all_gather(pshort, "grp", axis=0, tiled=True),
        lax.all_gather(qshort, "grp", axis=0, tiled=True),
    )
    own_cols = group_pos * pair_rows + local_rows
    positive = (jnp.arange(group_rows)[None, :] == own_cols[:, None]).astype(jnp.float32)
    inner_scores = (
        jnp.dot(qshort, group_p.T, preferred_element_type=jnp.float32) * inverse_permutation
    )
    hard_score = (
        jnp.einsum("rd,rd->r", qshort, hard_p, preferred_element_type=jnp.float32)
        * inverse_permutation
    )
    totals = jnp.log(jnp.sum(jnp.exp(inner_scores), 1) + jnp.exp(hard_score))
    inner_w = (jnp.exp(inner_scores - totals[:, None]) - positive).astype(jnp.bfloat16)
    hard_w = jnp.exp(hard_score - totals).astype(jnp.bfloat16)
    unit_q = (
        jnp.dot(inner_w, group_p, preferred_element_type=jnp.float32)
        + hard_w.astype(jnp.float32)[:, None] * hard_p
    ) * factor
    query_grad = norm_back(queries, qscale, unit_q).astype(jnp.bfloat16)
    group_totals = lax.all_gather(totals, "grp", axis=0, tiled=True)
    scores = jnp.dot(group_q, pshort.T, preferred_element_type=jnp.float32) * inverse_permutation
    weight_factors = (jnp.exp(scores - group_totals[:, None]) - positive.T).astype(jnp.bfloat16)
    unit_p = jnp.dot(weight_factors.T, group_q, preferred_element_type=jnp.float32) * factor
    return_table = local_rows[:, None] == served_flat[None, :]
    own_terms = hard_w.astype(jnp.float32)[:, None] * qshort * factor
    term_slots = jnp.dot(
        slot_table.astype(jnp.float32),
        own_terms,
        precision=lax.Precision.HIGHEST,
        preferred_element_type=jnp.float32,
    )
    grad_terms = lax.all_to_all(
        term_slots.reshape(batch_count, capacity, embedding_dimension).astype(jnp.bfloat16),
        "batch",
        split_axis=0,
        concat_axis=0,
        tiled=True,
    ).astype(jnp.float32)
    spread = jnp.dot(
        return_table.astype(jnp.float32),
        grad_terms.reshape(slot_total, embedding_dimension),
        precision=lax.Precision.HIGHEST,
        preferred_element_type=jnp.float32,
    )
    passage_grad = norm_back(passages, pscale, unit_p + spread).astype(jnp.bfloat16)
    return (query_grad, passage_grad)


def local(queries, passages, hard_ids):
    pair_rows = queries.shape[0]
    query_grad, passage_grad, flags = exchange(hard_ids.reshape(1, pair_rows), queries, passages)
    return lax.cond(
        flags[0, 0] > 0,
        lambda: padded(queries, passages, hard_ids),
        lambda: (query_grad, passage_grad),
    )


def solution(mesh):
    in_specs = (P(("batch", "grp"), None), P(("batch", "grp"), None), P(("batch", "grp")))
    out_specs = (P(("batch", "grp"), None), P(("batch", "grp"), None))
    return jax.shard_map(local, mesh=mesh, in_specs=in_specs, out_specs=out_specs, check_vma=False)
```

time: 249 us -> 219 us (0.88)
  other arithmetic: 13.2 us -> 0 us
  Pallas kernels: 210 us -> 200 us
  local copies, waits for them, and re-layouts: 10.5 us -> 3.36 us
    pallas_call x1 -> x0, Pallas kernels: 26.4 us -> none  [column(): pl.pallas_call(column_kernel, out_shape=jax.ShapeDtypeStruct((PLANES * PL...]
    pallas_call x1, Pallas kernels: 183 us -> 200 us  [exchange(): pl.pallas_call(exchange_kernel, out_shape=(jax.ShapeDtypeStruct((rows, wi...]
    reduce_sum x7 -> x0, other arithmetic: 6.17 us -> none  [the longest x1 2.3 us: too_many(): need = jnp.sum(uses.astype(jnp.int32), 2)]
    select_n x13 -> x0, other arithmetic: 3.51 us -> none  [the longest x1 1.46 us: course(): jnp.where(ahead == 0, 2, jnp.where(ahead < FAR, 0, jnp.where(ahead == FAR...]
    unnamed x18 -> x8, local copies, waits for them, and re-layouts: 6 us -> 3.36 us
where the time goes in v3:
time: 219 us
  Pallas kernels  200 us (91%)
  between operations  14.7 us (7%)
  local copies, waits for them, and re-layouts  3.36 us (2%)
    pallas_call x1, Pallas kernels, exchange(): pl.pallas_call(exchange_kernel, out_shape=(jax.ShapeDtypeStruct((rows, wi...  200 us

profile of v3, /device:TPU:1, one launch (start us, length us, event | category | flops | bytes accessed | tf_op | source)
XLA Modules:
  0.0 218.8 jit_solution(15970175855974149492)
XLA Ops:
  7.2 0.0 copy-start.2
  7.2 0.0 copy-start.9
  7.2 200.5 %exchange.1 = (bf16[128,4096]{1,0:T(8,128)(2,1)}, bf16[128,4096]{1,0:T(8,128)(2,1)}, f32[1,128]{1,0:T(1,128)}) custom-call(s32[1,128]{1,0:T(1,128)} %bitcast.21, bf16[128,4096]{1,0:T(8,128)(2,1)} %queries.1, bf16[128,4096]{1,0:T(8,128)(2,1)} %passages.1), custom_call_target="tpu_custom_call" | custom-call | flops 2147483648 | bytes 8388608 | tf_op jit(solution)/shard_map/exchange/pallas_call | solution.py:620
  208.4 0.0 copy-done.2
  208.4 0.0 copy-done.9
  208.4 0.3 conditional.1
  208.6 0.0 copy-start.8
  208.7 2.4 %copy.22 = bf16[128,4096]{1,0:T(8,128)(2,1)} copy(bf16[128,4096]{1,0:T(8,128)(2,1)} %get-tuple-element.49) | data formatting | bytes 2097152
  211.0 0.0 copy-done.8
  211.0 1.0 copy.23
Async XLA Ops:
  7.2 201.2 %copy-start.2 = (bf16[128,4096]{1,0:T(8,128)(2,1)S(1)}, bf16[128,4096]{1,0:T(8,128)(2,1)}, u32[]{:S(2)}) copy-start(bf16[128,4096]{1,0:T(8,128)(2,1)} %passages.1) | copy-start | bytes 3145732
  7.2 201.2 %copy-start.9 = (s32[128]{0:T(128)S(1)}, s32[128]{0:T(128)}, u32[]{:S(2)}) copy-start(s32[128]{0:T(128)} %param.7) | copy-start | bytes 1540
  208.6 2.4 %copy-start.8 = (bf16[128,4096]{1,0:T(8,128)(2,1)S(1)}, bf16[128,4096]{1,0:T(8,128)(2,1)}, u32[]{:S(2)}) copy-start(bf16[128,4096]{1,0:T(8,128)(2,1)} %get-tuple-element.50) | copy-start | bytes 3145732

commit v4 on v3

--- a/solution.py
+++ b/solution.py
@@ -16,7 +16,7 @@
 FAR = PLANES // 2
 SLOTS = 2
 OWN = PLANE * SLOTS
-CAPS = [0, 84, 76, 68, 60, 50, 38, 24, 8, 0]
+CAPS = [0, 82, 74, 67, 58, 48, 37, 24, 8, 0]
 LANES = 128
 Q_AT = {1: (2,), 3: (3,), 5: (4,), 6: (5,), 7: (6,)}
 
@@ -43,7 +43,7 @@
 
 OUT_AT, OUT_ROWS = offsets_of([0] + [CAPS[d] for d in range(1, FAR + 1)])
 CAP1 = CAPS[1]
-SPLIT = 40
+SPLIT = 128
 
 
 def parts_of(d):

time: 219 us -> 217 us (level)
    pallas_call x1, Pallas kernels: 200 us -> 198 us  [exchange(): pl.pallas_call(exchange_kernel, out_shape=(jax.ShapeDtypeStruct((rows, wi...]
where the time goes in v4:
time: 217 us; the launch traced here: 216 us
  Pallas kernels  198 us (91%)
  between operations  14.7 us (7%)
  local copies, waits for them, and re-layouts  3.36 us (2%)
    pallas_call x1, Pallas kernels, exchange(): pl.pallas_call(exchange_kernel, out_shape=(jax.ShapeDtypeStruct((rows, wi...  198 us

profile of v4, /device:TPU:1, one launch (start us, length us, event | category | flops | bytes accessed | tf_op | source)
XLA Modules:
  0.0 216.4 jit_solution(2394953010811050775)
XLA Ops:
  7.2 0.0 copy-start.2
  7.2 0.0 copy-start.9
  7.2 198.1 %exchange.1 = (bf16[128,4096]{1,0:T(8,128)(2,1)}, bf16[128,4096]{1,0:T(8,128)(2,1)}, f32[1,128]{1,0:T(1,128)}) custom-call(s32[1,128]{1,0:T(1,128)} %bitcast.21, bf16[128,4096]{1,0:T(8,128)(2,1)} %queries.1, bf16[128,4096]{1,0:T(8,128)(2,1)} %passages.1), custom_call_target="tpu_custom_call" | custom-call | flops 2147483648 | bytes 8388608 | tf_op jit(solution)/shard_map/exchange/pallas_call | solution.py:620
  205.9 0.0 copy-done.2
  205.9 0.0 copy-done.9
  206.0 0.3 conditional.1
  206.2 0.0 copy-start.8
  206.2 2.4 %copy.22 = bf16[128,4096]{1,0:T(8,128)(2,1)} copy(bf16[128,4096]{1,0:T(8,128)(2,1)} %get-tuple-element.49) | data formatting | bytes 2097152
  208.6 0.0 copy-done.8
  208.6 1.0 copy.23
Async XLA Ops:
  7.2 198.8 %copy-start.2 = (bf16[128,4096]{1,0:T(8,128)(2,1)S(1)}, bf16[128,4096]{1,0:T(8,128)(2,1)}, u32[]{:S(2)}) copy-start(bf16[128,4096]{1,0:T(8,128)(2,1)} %passages.1) | copy-start | bytes 3145732
  7.2 198.8 %copy-start.9 = (s32[128]{0:T(128)S(1)}, s32[128]{0:T(128)}, u32[]{:S(2)}) copy-start(s32[128]{0:T(128)} %param.7) | copy-start | bytes 1540
  206.2 2.4 %copy-start.8 = (bf16[128,4096]{1,0:T(8,128)(2,1)S(1)}, bf16[128,4096]{1,0:T(8,128)(2,1)}, u32[]{:S(2)}) copy-start(bf16[128,4096]{1,0:T(8,128)(2,1)} %get-tuple-element.50) | copy-start | bytes 3145732
